TPU v7x, 32 devices: a whole 2x2x4 slice. The times are simulated.
32 devices in a mesh: rep: 4 (over y, core), fsdp: 8 (over z, x).
Axes of the slice: x: 2, y: 2, z: 4, core: 2. Of those that a mesh axis runs over, the one named last changes fastest.
Arguments:
- tokens: bfloat16 [16384, 1024], P(('rep', 'fsdp')), may hold values from -6 to 6
- segment: int32 [16384], P(('rep', 'fsdp')), may hold values from -1 to 9, as said below
- cotangent: bfloat16 [16384, 1024], P(('rep', 'fsdp')), may hold values from -6 to 6
- attn_norm_gain: bfloat16 [1024], P('fsdp'), may hold values from 0.5 to 1.5
- attn_norm_bias: bfloat16 [1024], P('fsdp'), may hold values from -1.75 to 1.75
- qkv_weight: bfloat16 [1024, 3072], P('fsdp'), may hold values from -0.1875 to 0.1875
- query_bias: bfloat16 [1024], P('fsdp'), may hold values from -3 to 3
- value_bias: bfloat16 [1024], P('fsdp'), may hold values from -3 to 3
- proj_weight: bfloat16 [1024, 1024], P('fsdp'), may hold values from -4 to 4
- proj_bias: bfloat16 [1024], P('fsdp'), may hold values from -1.75 to 1.75
- attn_scale: bfloat16 [1024], P('fsdp'), may hold values from 0.29882812 to 1.5
- mlp_norm_gain: bfloat16 [1024], P('fsdp'), may hold values from 0.5 to 1.5
- mlp_norm_bias: bfloat16 [1024], P('fsdp'), may hold values from -1.75 to 1.75
- hidden_weight: bfloat16 [1024, 4096], P('fsdp'), may hold values from -0.1875 to 0.1875
- hidden_bias: bfloat16 [4096], P('fsdp'), may hold values from -1.75 to 1.75
- output_weight: bfloat16 [4096, 1024], P('fsdp'), may hold values from -0.09375 to 0.09375
- output_bias: bfloat16 [1024], P('fsdp'), may hold values from -1.75 to 1.75
- mlp_scale: bfloat16 [1024], P('fsdp'), may hold values from 0.29882812 to 1.5
Outputs:
- block_output: bfloat16 [16384, 1024], P(('rep', 'fsdp'))
- input_grad: float32 [16384, 1024], P(('rep', 'fsdp'))
- attn_norm_gain_grad: float32 [1024], P('fsdp')
- attn_norm_bias_grad: float32 [1024], P('fsdp')
- qkv_weight_grad: float32 [1024, 3072], P('fsdp')
- query_bias_grad: float32 [1024], P('fsdp')
- value_bias_grad: float32 [1024], P('fsdp')
- proj_weight_grad: float32 [1024, 1024], P('fsdp')
- proj_bias_grad: float32 [1024], P('fsdp')
- attn_scale_grad: float32 [1024], P('fsdp')
- mlp_norm_gain_grad: float32 [1024], P('fsdp')
- mlp_norm_bias_grad: float32 [1024], P('fsdp')
- hidden_weight_grad: float32 [1024, 4096], P('fsdp')
- hidden_bias_grad: float32 [4096], P('fsdp')
- output_weight_grad: float32 [4096, 1024], P('fsdp')
- output_bias_grad: float32 [1024], P('fsdp')
- mlp_scale_grad: float32 [1024], P('fsdp')
Inputs may be any that keep to these rules, and one draw needn't show every extreme that they name: `segment`: image k (0 to 9) is a run of exactly 1370 consecutive tokens that starts after image k - 1 ends; -1 marks padding tokens between the images; image 0 starts at token 0; some image starts at the last token of a device's rows, so it extends 3 devices further; the last image starts at token 14847.
All inputs are finite; a program needn't handle non-finite values.
Results may differ from a plain program's by a relative error of at most 0.02.
Values may be sent and summed in bfloat16 or wider, within the bound.
A program may use at most 256 MiB of HBM per device.

v0:
```python
import jax
import jax.numpy as jnp
from jax import lax
from jax.sharding import PartitionSpec as P

H = 16
HD = 64
REACH = 3


EPS = 1e-06
NEG = -1e30


def passed_along(value, axis, steps):
    count = lax.axis_size(axis)
    leading, last = (max(0, -steps), min(count, count - steps))
    return lax.ppermute(value, axis, [(source, source + steps) for source in range(leading, last)])


def layer_norm(matrix):
    average = jnp.mean(matrix, axis=-1, keepdims=True)
    centred = matrix - average
    second_moment = jnp.mean(centred * centred, axis=-1, keepdims=True)
    return centred * lax.rsqrt(second_moment + EPS)


def gelu_exact(values):
    return jax.nn.gelu(values, approximate=False)


def plain_dot(first_op, second_op):
    return jnp.dot(first_op, second_op, preferred_element_type=jnp.float32)


def dot_first_t(first_op, second_op):
    return lax.dot_general(
        first_op, second_op, (((0,), (0,)), ((), ())), preferred_element_type=jnp.float32
    )


def dot_second_t(first_op, second_op):
    return lax.dot_general(
        first_op, second_op, (((1,), (1,)), ((), ())), preferred_element_type=jnp.float32
    )


def column_sum(matrix):
    return jnp.sum(matrix.astype(jnp.float32), axis=0)


def as_float(vector):
    return vector.astype(jnp.float32)


def heads_first(matrix):
    return matrix.reshape(matrix.shape[0], H, HD).transpose(1, 0, 2)


def heads_last(stacked):
    return stacked.transpose(1, 0, 2).reshape(stacked.shape[1], H * HD)


def side_offsets():
    return [offset for offset in range(-REACH, REACH + 1) if offset != 0]


def side_lists(mover):
    row_list = []
    code_list = []
    for offset in side_offsets():
        moved_rows, moved_codes = mover(-offset)
        row_list.append(moved_rows)
        code_list.append(moved_codes)
    return (row_list, code_list)


def assemble(center_rows, center_codes, side_rows, side_codes):
    row_blocks = side_rows[:REACH] + [center_rows] + side_rows[REACH:]
    code_blocks = side_codes[:REACH] + [center_codes] + side_codes[REACH:]
    return (jnp.concatenate(row_blocks, axis=0), jnp.concatenate(code_blocks, axis=0))


def allowed_pairs(own_codes, near_codes):
    tok_rows = own_codes.shape[0]
    key_count = near_codes.shape[0]
    row_at = lax.broadcasted_iota(jnp.int32, (tok_rows, key_count), 0)
    col_at = lax.broadcasted_iota(jnp.int32, (tok_rows, key_count), 1)
    same_image = (own_codes[:, None] == near_codes[None, :]) & (near_codes[None, :] >= 2)
    return same_image | (row_at + REACH * tok_rows == col_at)


def local(
    tokens,
    segment,
    cotangent,
    attn_norm_gain,
    attn_norm_bias,
    qkv_weight,
    query_bias,
    value_bias,
    proj_weight,
    proj_bias,
    attn_scale,
    mlp_norm_gain,
    mlp_norm_bias,
    hidden_weight,
    hidden_bias,
    output_weight,
    output_bias,
    mlp_scale,
):
    gathered = (
        lax.all_gather(attn_norm_gain, "fsdp", axis=0, tiled=True),
        lax.all_gather(attn_norm_bias, "fsdp", axis=0, tiled=True),
        lax.all_gather(qkv_weight, "fsdp", axis=0, tiled=True),
        lax.all_gather(query_bias, "fsdp", axis=0, tiled=True),
        lax.all_gather(value_bias, "fsdp", axis=0, tiled=True),
        lax.all_gather(proj_weight, "fsdp", axis=0, tiled=True),
        lax.all_gather(proj_bias, "fsdp", axis=0, tiled=True),
        lax.all_gather(attn_scale, "fsdp", axis=0, tiled=True),
        lax.all_gather(mlp_norm_gain, "fsdp", axis=0, tiled=True),
        lax.all_gather(mlp_norm_bias, "fsdp", axis=0, tiled=True),
        lax.all_gather(hidden_weight, "fsdp", axis=0, tiled=True),
        lax.all_gather(hidden_bias, "fsdp", axis=0, tiled=True),
        lax.all_gather(output_weight, "fsdp", axis=0, tiled=True),
        lax.all_gather(output_bias, "fsdp", axis=0, tiled=True),
        lax.all_gather(mlp_scale, "fsdp", axis=0, tiled=True),
    )
    (
        gain_one,
        shift_one,
        w_qkv,
        bias_query,
        bias_value,
        w_proj,
        bias_proj,
        scale_one,
        gain_two,
        shift_two,
        w_hidden,
        bias_hidden,
        w_output,
        bias_output,
        scale_two,
    ) = gathered
    model_width = tokens.shape[1]
    tok_rows = tokens.shape[0]
    score_scale = HD ** (-0.5)
    inputs = tokens.astype(jnp.float32)
    normed_one = layer_norm(inputs)
    first_in = (normed_one * as_float(gain_one) + as_float(shift_one)).astype(jnp.bfloat16)
    kv_bias = jnp.concatenate([jnp.zeros((model_width,), jnp.float32), as_float(bias_value)])
    bias_row = jnp.concatenate([as_float(bias_query), kv_bias])
    mixed_qkv = (plain_dot(first_in, w_qkv) + bias_row).astype(jnp.bfloat16)
    queries = mixed_qkv[:, :model_width]
    packed = mixed_qkv[:, model_width:]
    image_codes = segment + 2
    side_rows, side_codes = side_lists(
        lambda shift_by: passed_along((packed, image_codes), ("rep", "fsdp"), shift_by)
    )
    near_rows, near_codes = assemble(packed, image_codes, side_rows, side_codes)
    allowed = allowed_pairs(image_codes, near_codes)

    def head_forward(operands):
        query_head, key_head, value_head = operands
        scores = jnp.where(allowed, dot_second_t(query_head, key_head) * score_scale, NEG)
        row_peak = jnp.max(scores, axis=1, keepdims=True)
        weights = jnp.exp(scores - row_peak)
        row_total = jnp.sum(weights, axis=1, keepdims=True)
        probability = weights / row_total
        return (plain_dot(probability.astype(jnp.bfloat16), value_head), row_peak, row_total)

    query_heads = heads_first(queries)
    key_heads = heads_first(near_rows[:, :model_width])
    value_heads = heads_first(near_rows[:, model_width:])
    head_out, peaks, totals = lax.map(head_forward, (query_heads, key_heads, value_heads))
    attended = heads_last(head_out).astype(jnp.bfloat16)
    branch_one = plain_dot(attended, w_proj) + as_float(bias_proj)
    middle = inputs + as_float(scale_one) * branch_one
    normed_two = layer_norm(middle)
    second_in = (normed_two * as_float(gain_two) + as_float(shift_two)).astype(jnp.bfloat16)
    hidden = plain_dot(second_in, w_hidden) + as_float(bias_hidden)
    active = gelu_exact(hidden).astype(jnp.bfloat16)
    branch_two = plain_dot(active, w_output) + as_float(bias_output)
    block_output = (middle + as_float(scale_two) * branch_two).astype(jnp.bfloat16)
    weights_again = (
        lax.all_gather(attn_norm_gain, "fsdp", axis=0, tiled=True),
        lax.all_gather(attn_norm_bias, "fsdp", axis=0, tiled=True),
        lax.all_gather(qkv_weight, "fsdp", axis=0, tiled=True),
        lax.all_gather(query_bias, "fsdp", axis=0, tiled=True),
        lax.all_gather(value_bias, "fsdp", axis=0, tiled=True),
        lax.all_gather(proj_weight, "fsdp", axis=0, tiled=True),
        lax.all_gather(proj_bias, "fsdp", axis=0, tiled=True),
        lax.all_gather(attn_scale, "fsdp", axis=0, tiled=True),
        lax.all_gather(mlp_norm_gain, "fsdp", axis=0, tiled=True),
        lax.all_gather(mlp_norm_bias, "fsdp", axis=0, tiled=True),
        lax.all_gather(hidden_weight, "fsdp", axis=0, tiled=True),
        lax.all_gather(hidden_bias, "fsdp", axis=0, tiled=True),
        lax.all_gather(output_weight, "fsdp", axis=0, tiled=True),
        lax.all_gather(output_bias, "fsdp", axis=0, tiled=True),
        lax.all_gather(mlp_scale, "fsdp", axis=0, tiled=True),
    )
    (
        gain_one,
        shift_one,
        w_qkv,
        bias_query,
        bias_value,
        w_proj,
        bias_proj,
        scale_one,
        gain_two,
        shift_two,
        w_hidden,
        bias_hidden,
        w_output,
        bias_output,
        scale_two,
    ) = weights_again
    w_query = w_qkv[:, :model_width]
    w_kv = w_qkv[:, model_width:]
    upstream = cotangent.astype(jnp.float32)
    scale_two_grad = jnp.sum(upstream * branch_two, axis=0)
    g_branch_two = (as_float(scale_two) * upstream).astype(jnp.bfloat16)
    output_weight_grad = dot_first_t(active, g_branch_two)
    output_bias_grad = column_sum(g_branch_two)
    g_active = dot_second_t(g_branch_two, w_output)
    gelu_value, gelu_pull = jax.vjp(gelu_exact, hidden)
    g_hidden = gelu_pull(g_active)[0].astype(jnp.bfloat16)
    hidden_weight_grad = dot_first_t(second_in, g_hidden)
    hidden_bias_grad = column_sum(g_hidden)
    g_second = dot_second_t(g_hidden, w_hidden)
    gain_two_grad = jnp.sum(g_second * normed_two, axis=0)
    shift_two_grad = jnp.sum(g_second, axis=0)
    norm_value_two, norm_pull_two = jax.vjp(layer_norm, middle)
    g_middle = upstream + norm_pull_two(g_second * as_float(gain_two))[0]
    scale_one_grad = jnp.sum(g_middle * branch_one, axis=0)
    g_branch_one = (as_float(scale_one) * g_middle).astype(jnp.bfloat16)
    proj_weight_grad = dot_first_t(attended, g_branch_one)
    proj_bias_grad = column_sum(g_branch_one)
    g_attended = dot_second_t(g_branch_one, w_proj).astype(jnp.bfloat16)
    side_rows, side_codes = side_lists(
        lambda shift_by: passed_along((packed, image_codes), ("rep", "fsdp"), shift_by)
    )
    rows_again, codes_again = assemble(packed, image_codes, side_rows, side_codes)
    allowed_again = allowed_pairs(image_codes, codes_again)
    key_heads = heads_first(rows_again[:, :model_width])
    value_heads = heads_first(rows_again[:, model_width:])

    def head_backward(operands):
        query_head, key_head, value_head, grad_head, peak_head, total_head = operands
        scores = jnp.where(allowed_again, dot_second_t(query_head, key_head) * score_scale, NEG)
        probability = jnp.exp(scores - peak_head) / total_head
        prob_low = probability.astype(jnp.bfloat16)
        g_probs = dot_second_t(grad_head, value_head)
        row_inner = jnp.sum(g_probs * probability, axis=1, keepdims=True)
        g_scores = (probability * (g_probs - row_inner)).astype(jnp.bfloat16)
        g_query_head = plain_dot(g_scores, key_head) * score_scale
        g_key_head = dot_first_t(g_scores, query_head) * score_scale
        g_value_head = dot_first_t(prob_low, grad_head)
        return (g_query_head, g_key_head, g_value_head)

    g_query, g_keys, g_values = lax.map(
        head_backward, (query_heads, key_heads, value_heads, heads_first(g_attended), peaks, totals)
    )
    g_query_low = heads_last(g_query).astype(jnp.bfloat16)
    g_near = jnp.concatenate([heads_last(g_keys), heads_last(g_values)], axis=1).astype(
        jnp.bfloat16
    )
    own_piece = g_near[REACH * tok_rows : (REACH + 1) * tok_rows]
    offsets = side_offsets()
    side_pieces = [
        g_near[(offset + REACH) * tok_rows : (offset + REACH + 1) * tok_rows] for offset in offsets
    ]
    query_weight_grad = dot_first_t(first_in, g_query_low)
    query_bias_grad = column_sum(g_query_low)
    kv_weight_grad = dot_first_t(first_in, own_piece)
    value_bias_grad = column_sum(own_piece[:, model_width:])
    g_first = dot_second_t(g_query_low, w_query) + dot_second_t(own_piece, w_kv)
    arrived = []
    for index, offset in enumerate(offsets):
        arrived.append(passed_along(side_pieces[index], ("rep", "fsdp"), offset))
    arrived_stack = jnp.concatenate(arrived, axis=0)
    kv_weight_grad = kv_weight_grad + dot_first_t(
        jnp.concatenate([first_in] * len(offsets), axis=0), arrived_stack
    )
    value_bias_grad = value_bias_grad + column_sum(arrived_stack[:, model_width:])
    arrived_first = dot_second_t(arrived_stack, w_kv)
    g_first = g_first + jnp.sum(arrived_first.reshape(len(offsets), tok_rows, model_width), axis=0)
    qkv_weight_grad = jnp.concatenate([query_weight_grad, kv_weight_grad], axis=1)
    gain_one_grad = jnp.sum(g_first * normed_one, axis=0)
    shift_one_grad = jnp.sum(g_first, axis=0)
    norm_value_one, norm_pull_one = jax.vjp(layer_norm, inputs)
    input_grad = g_middle + norm_pull_one(g_first * as_float(gain_one))[0]
    summed = (
        lax.psum_scatter(
            gain_one_grad.astype(jnp.bfloat16), "fsdp", scatter_dimension=0, tiled=True
        ).astype(jnp.float32),
        lax.psum_scatter(
            shift_one_grad.astype(jnp.bfloat16), "fsdp", scatter_dimension=0, tiled=True
        ).astype(jnp.float32),
        lax.psum_scatter(
            qkv_weight_grad.astype(jnp.bfloat16), "fsdp", scatter_dimension=0, tiled=True
        ).astype(jnp.float32),
        lax.psum_scatter(
            query_bias_grad.astype(jnp.bfloat16), "fsdp", scatter_dimension=0, tiled=True
        ).astype(jnp.float32),
        lax.psum_scatter(
            value_bias_grad.astype(jnp.bfloat16), "fsdp", scatter_dimension=0, tiled=True
        ).astype(jnp.float32),
        lax.psum_scatter(
            proj_weight_grad.astype(jnp.bfloat16), "fsdp", scatter_dimension=0, tiled=True
        ).astype(jnp.float32),
        lax.psum_scatter(
            proj_bias_grad.astype(jnp.bfloat16), "fsdp", scatter_dimension=0, tiled=True
        ).astype(jnp.float32),
        lax.psum_scatter(
            scale_one_grad.astype(jnp.bfloat16), "fsdp", scatter_dimension=0, tiled=True
        ).astype(jnp.float32),
        lax.psum_scatter(
            gain_two_grad.astype(jnp.bfloat16), "fsdp", scatter_dimension=0, tiled=True
        ).astype(jnp.float32),
        lax.psum_scatter(
            shift_two_grad.astype(jnp.bfloat16), "fsdp", scatter_dimension=0, tiled=True
        ).astype(jnp.float32),
        lax.psum_scatter(
            hidden_weight_grad.astype(jnp.bfloat16), "fsdp", scatter_dimension=0, tiled=True
        ).astype(jnp.float32),
        lax.psum_scatter(
            hidden_bias_grad.astype(jnp.bfloat16), "fsdp", scatter_dimension=0, tiled=True
        ).astype(jnp.float32),
        lax.psum_scatter(
            output_weight_grad.astype(jnp.bfloat16), "fsdp", scatter_dimension=0, tiled=True
        ).astype(jnp.float32),
        lax.psum_scatter(
            output_bias_grad.astype(jnp.bfloat16), "fsdp", scatter_dimension=0, tiled=True
        ).astype(jnp.float32),
        lax.psum_scatter(
            scale_two_grad.astype(jnp.bfloat16), "fsdp", scatter_dimension=0, tiled=True
        ).astype(jnp.float32),
    )
    owned = (
        lax.psum(summed[0].astype(jnp.bfloat16), "rep").astype(jnp.float32),
        lax.psum(summed[1].astype(jnp.bfloat16), "rep").astype(jnp.float32),
        lax.psum(summed[2].astype(jnp.bfloat16), "rep").astype(jnp.float32),
        lax.psum(summed[3].astype(jnp.bfloat16), "rep").astype(jnp.float32),
        lax.psum(summed[4].astype(jnp.bfloat16), "rep").astype(jnp.float32),
        lax.psum(summed[5].astype(jnp.bfloat16), "rep").astype(jnp.float32),
        lax.psum(summed[6].astype(jnp.bfloat16), "rep").astype(jnp.float32),
        lax.psum(summed[7].astype(jnp.bfloat16), "rep").astype(jnp.float32),
        lax.psum(summed[8].astype(jnp.bfloat16), "rep").astype(jnp.float32),
        lax.psum(summed[9].astype(jnp.bfloat16), "rep").astype(jnp.float32),
        lax.psum(summed[10].astype(jnp.bfloat16), "rep").astype(jnp.float32),
        lax.psum(summed[11].astype(jnp.bfloat16), "rep").astype(jnp.float32),
        lax.psum(summed[12].astype(jnp.bfloat16), "rep").astype(jnp.float32),
        lax.psum(summed[13].astype(jnp.bfloat16), "rep").astype(jnp.float32),
        lax.psum(summed[14].astype(jnp.bfloat16), "rep").astype(jnp.float32),
    )
    return (
        block_output,
        input_grad,
        owned[0],
        owned[1],
        owned[2],
        owned[3],
        owned[4],
        owned[5],
        owned[6],
        owned[7],
        owned[8],
        owned[9],
        owned[10],
        owned[11],
        owned[12],
        owned[13],
        owned[14],
    )


def solution(mesh):
    return jax.shard_map(
        local,
        mesh=mesh,
        in_specs=(
            P(("rep", "fsdp"), None),
            P(("rep", "fsdp")),
            P(("rep", "fsdp"), None),
            P("fsdp"),
            P("fsdp"),
            P("fsdp", None),
            P("fsdp"),
            P("fsdp"),
            P("fsdp", None),
            P("fsdp"),
            P("fsdp"),
            P("fsdp"),
            P("fsdp"),
            P("fsdp", None),
            P("fsdp"),
            P("fsdp", None),
            P("fsdp"),
            P("fsdp"),
        ),
        out_specs=(
            P(("rep", "fsdp"), None),
            P(("rep", "fsdp"), None),
            P("fsdp"),
            P("fsdp"),
            P("fsdp", None),
            P("fsdp"),
            P("fsdp"),
            P("fsdp", None),
            P("fsdp"),
            P("fsdp"),
            P("fsdp"),
            P("fsdp"),
            P("fsdp", None),
            P("fsdp"),
            P("fsdp", None),
            P("fsdp"),
            P("fsdp"),
        ),
        check_vma=False,
    )
```

profile of v0, /device:TPU:0, one launch (start us, length us, event | category | flops | bytes accessed | tf_op | source)
XLA Modules:
  0.0 2194.2 jit_solution(10285854938416718432)
XLA Ops:
  9.5 22.5 %all-gather.1 = bf16[8,1,128]{2,1,0:T(2,128)(2,1)S(1)} all-gather(bf16[1,1,128]{2,1,0:T(2,128)(2,1)} %bitcast.226), channel_id=1, replica_groups=mesh['rep'=4,'fsdp'=8] {'fsdp'}, dimensions={0}, use_global_device_ids=true | all-gather | bytes 2304 | tf_op jit(solution)/shard_map/all_gather | solution.py:114
  32.0 16.7 all-gather.2
  48.7 18.4 all-gather.3
  67.1 16.8 all-gather.4
  87.6 24.5 %all-gather.16.cloned.1.call-done = bf16[1024,3072]{1,0:T(8,128)(2,1)} async-done(((bf16[128,3072]{1,0:T(8,128)(2,1)}), bf16[1024,3072]{1,0:T(8,128)(2,1)}) %all-gather.16.cloned.1.call-update) | async-done | bytes 6291472 | tf_op jit(solution)/shard_map/all_gather | solution.py:116
  112.1 6.7 add_convert_fusion.2
  124.1 5.3 collective-permute-start.1
  136.6 141.2 %all-gather = bf16[8,1,128]{2,1,0:T(2,128)(2,1)S(1)} all-gather(bf16[1,1,128]{2,1,0:T(2,128)(2,1)S(1)} %bitcast.230), channel_id=1, replica_groups=mesh['rep'=4,'fsdp'=8] {'fsdp'}, dimensions={0}, use_global_device_ids=true | all-gather | bytes 2304 | tf_op jit(solution)/shard_map/all_gather | solution.py:121
  277.9 109.3 %all-gather.5 = bf16[8,1,128]{2,1,0:T(2,128)(2,1)S(1)} all-gather(bf16[1,1,128]{2,1,0:T(2,128)(2,1)S(1)} %bitcast.231), channel_id=1, replica_groups=mesh['rep'=4,'fsdp'=8] {'fsdp'}, dimensions={0}, use_global_device_ids=true | all-gather | bytes 2304 | tf_op jit(solution)/shard_map/all_gather | solution.py:120
  387.2 16.4 all-gather.7
  403.6 26.4 %all-gather.9 = bf16[8,1,512]{2,1,0:T(2,128)(2,1)S(1)} all-gather(bf16[1,1,512]{2,1,0:T(2,128)(2,1)S(1)} %reshape.210), channel_id=1, replica_groups=mesh['rep'=4,'fsdp'=8] {'fsdp'}, dimensions={0}, use_global_device_ids=true | all-gather | bytes 9216 | tf_op jit(solution)/shard_map/all_gather | solution.py:125
  430.1 17.1 all-gather.8
  447.2 17.5 all-gather.6
  476.4 6.2 collective-permute-done.11
  495.2 28.2 %collective-permute-done.3 = bf16[512,2048]{1,0:T(8,128)(2,1)} collective-permute-done((bf16[512,2048]{1,0:T(8,128)(2,1)}, bf16[512,2048]{1,0:T(8,128)(2,1)}, u32[]{:S(2)}, u32[]{:S(2)}) %collective-permute-start.3) | collective-permute-done | bytes 2097184 | tf_op jit(solution)/shard_map/ppermute | solution.py:18
  525.3 119.6 %collective-permute-done.4 = bf16[512,2048]{1,0:T(8,128)(2,1)} collective-permute-done((bf16[512,2048]{1,0:T(8,128)(2,1)}, bf16[512,2048]{1,0:T(8,128)(2,1)}, u32[]{:S(2)}, u32[]{:S(2)}) %collective-permute-start.4) | collective-permute-done | bytes 2097184 | tf_op jit(solution)/shard_map/ppermute | solution.py:18
  646.7 50.4 %collective-permute-done.5 = bf16[512,2048]{1,0:T(8,128)(2,1)} collective-permute-done((bf16[512,2048]{1,0:T(8,128)(2,1)}, bf16[512,2048]{1,0:T(8,128)(2,1)}, u32[]{:S(2)}, u32[]{:S(2)}) %collective-permute-start.5) | collective-permute-done | bytes 2097184 | tf_op jit(solution)/shard_map/ppermute | solution.py:18
  698.9 5.7 fusion.99
  704.7 10.0 copy.53
  714.7 13.8 copy.56
  728.5 10.0 copy.54
  738.5 13.8 copy.57
  752.4 131.8 %while.30 = (s32[]{:T(128)}, bf16[16,512,64]{1,2,0:T(8,128)(2,1)S(1)}, f32[16,512,1]{1,2,0:T(1,128)S(1)}, f32[16,512,1]{1,2,0:T(1,128)S(1)}, bf16[16,512,64]{2,1...) while((s32[]{:T(128)}, ...), condition=%wide.region_5.6_spmd.clone, body=%wide.region_2.5_spmd.clone.sunk | while | flops 491781120 | bytes 24159864 | solution.py:177
  890.2 28.1 %multiply_convert_fusion.1 = (bf16[512,4096]{1,0:T(8,128)(2,1)}, f32[512,4096]{1,0:T(8,128)}, f32[512,4096]{1,0:T(8,128)}) fusion(f32[4096]{0:T(1024)S(1)} %bitcast.213, bf16[1024,4096]{1,0:T(8,128)(2,1)} %all-gather.20.cloned.1.call-done, f32[512,1024]{1,0:T(8,128)S(1)} %get-tuple-element.330, f32[1024]{0:T(1024)S(1)} %bitcast.223, ...), kind=kOutput, calls=%fused_computation.74 | convolution fusion | flops 4436000768 | bytes 31485952 | tf_op jit(solution)/shard_map/dot_general | solution.py:33
  918.3 15.4 fusion.100
  933.7 8.0 multiply_reduce_fusion.1
  947.8 364.0 %while.31 = (s32[]{:T(128)}, bf16[16,512,64]{1,2,0:T(8,128)(2,1)S(1)}, bf16[16,3584,64]{1,2,0:T(8,128)(2,1)}, bf16[16,3584,64]{1,2,0:T(8,128)(2,1)}, bf16[16,512...) while((s32[]{:T(128)}, ...), condition=%wide.region_12.13_spmd.clone, body=%wide.region_10.12_spmd.clone.sunk | while | flops 1200356864 | bytes 68594376 | solution.py:264
  953.0 5.2 multiply_reduce_fusion.6
  975.8 5.2 multiply_reduce_fusion.6
  998.5 5.2 multiply_reduce_fusion.6
  1021.3 5.2 multiply_reduce_fusion.6
  1044.0 5.2 multiply_reduce_fusion.6
  1066.8 5.2 multiply_reduce_fusion.6
  1089.5 5.2 multiply_reduce_fusion.6
  1112.3 5.2 multiply_reduce_fusion.6
  1135.0 5.2 multiply_reduce_fusion.6
  1157.7 5.2 multiply_reduce_fusion.6
  1180.5 5.2 multiply_reduce_fusion.6
  1203.3 5.2 multiply_reduce_fusion.6
  1226.1 5.2 multiply_reduce_fusion.6
  1248.8 5.2 multiply_reduce_fusion.6
  1271.6 5.2 multiply_reduce_fusion.6
  1311.9 10.2 pad_maximum_fusion.1
  1333.5 44.8 %collective-permute-start.15 = (bf16[512,2048]{0,1:T(8,128)(2,1)}, bf16[512,2048]{0,1:T(8,128)(2,1)}, u32[]{:S(2)}, u32[]{:S(2)}) collective-permute-start(bf16[512,2048]{0,1:T(8,128)(2,1)} %get-tuple-element.343), channel_id=1, source_target_pairs={{0,1},{1,2},{2,3},{3,4},{4,5},{5,6},{6,7},{7,8},{8,9},{9,10},{10,1... | collective-permute-start | bytes 6291464 | tf_op jit(solution)/shard_map/ppermute | solution.py:18
  1390.0 6.4 collective-permute-start.17
  1400.6 7.5 fusion.87
  1411.3 11.9 collective-permute-done.13
  1426.4 37.3 %collective-permute-done.14 = bf16[512,2048]{0,1:T(8,128)(2,1)} collective-permute-done((bf16[512,2048]{0,1:T(8,128)(2,1)}, bf16[512,2048]{0,1:T(8,128)(2,1)}, u32[]{:S(2)}, u32[]{:S(2)}) %collective-permute-start.14) | collective-permute-done | bytes 2097184 | tf_op jit(solution)/shard_map/ppermute | solution.py:18
  1466.9 36.7 %collective-permute-done.15 = bf16[512,2048]{0,1:T(8,128)(2,1)} collective-permute-done((bf16[512,2048]{0,1:T(8,128)(2,1)}, bf16[512,2048]{0,1:T(8,128)(2,1)}, u32[]{:S(2)}, u32[]{:S(2)}) %collective-permute-start.15) | collective-permute-done | bytes 2097184 | tf_op jit(solution)/shard_map/ppermute | solution.py:18
  1513.2 20.6 add_convert_fusion
  1533.8 5.3 pad_maximum_fusion
  1540.7 9.2 convolution_convert_fusion.1
  1551.1 9.0 convolution_convert_fusion
  1560.7 127.7 %all-gather.10 = bf16[8,1,128]{2,1,0:T(2,128)(2,1)S(1)} all-gather(bf16[1,1,128]{2,1,0:T(2,128)(2,1)S(1)} %bitcast.235), channel_id=1, replica_groups=mesh['rep'=4,'fsdp'=8] {'fsdp'}, dimensions={0}, use_global_device_ids=true | all-gather | bytes 2304 | tf_op jit(solution)/shard_map/all_gather | solution.py:127
  1696.4 19.3 fusion.50
  1715.7 8.0 reduce_sum.259
  1723.7 6.9 fusion.93
  1735.5 69.4 %reduce-scatter.5.cloned.1.call-done = bf16[128,3072]{1,0:T(8,128)(2,1)} async-done(((bf16[1024,3072]{1,0:T(8,128)(2,1)}), bf16[128,3072]{1,0:T(8,128)(2,1)}) %reduce-scatter.5.cloned.1.call-update) | async-done | bytes 786448 | tf_op jit(solution)/shard_map/reduce_scatter | solution.py:303
  1804.9 151.8 %reduce-scatter.9.cloned.1.call-done = bf16[128,4096]{1,0:T(8,128)(2,1)} async-done(((bf16[1024,4096]{1,0:T(8,128)(2,1)}), bf16[128,4096]{1,0:T(8,128)(2,1)}) %reduce-scatter.9.cloned.1.call-update) | async-done | bytes 1048592 | tf_op jit(solution)/shard_map/reduce_scatter | solution.py:327
  1956.7 152.1 %reduce-scatter.11.cloned.1.call-done = bf16[512,1024]{1,0:T(8,128)(2,1)} async-done(((bf16[4096,1024]{1,0:T(8,128)(2,1)}), bf16[512,1024]{1,0:T(8,128)(2,1)}) %reduce-scatter.11.cloned.1.call-update) | async-done | bytes 1048592 | tf_op jit(solution)/shard_map/reduce_scatter | solution.py:333
  2108.9 13.7 fusion.66
  2122.6 35.2 %all-reduce.11 = (bf16[1024]{0:T(1024)(128)(2,1)S(1)}, bf16[1024]{0:T(1024)(128)(2,1)S(1)}, bf16[1024]{0:T(1024)(128)(2,1)S(1)}, bf16[1024]{0:T(1024)(128)(2,1)S...) all-reduce(bf16[1024]{0:T(1024)(128)(2,1)S(1)} %get-tuple-element.2, ...), channel_id=2, replica_groups=mesh['rep'=4,'fsdp'=8] {'fsdp'}, use_global_device_ids=true, to_apply=%region_17.18.clone | all-reduce | flops 14336 | bytes 57344
  2158.6 6.4 all-reduce.12
  2170.7 8.9 all-reduce.16.cloned.1.call-done
  (493 shorter events, 551.7 us)
Async XLA Ops:
  7.2 104.9 %copy-start = (bf16[512,1024]{1,0:T(8,128)(2,1)S(1)}, bf16[512,1024]{1,0:T(8,128)(2,1)}, u32[]{:S(2)}) copy-start(bf16[512,1024]{1,0:T(8,128)(2,1)} %param.22) | copy-start | bytes 3145732
  7.2 104.9 %all-gather.16.cloned.1.call-start = ((), (), s32[]{:S(2)}) async-start(), calls=%async_computation.4 | async-start | bytes 7077888 | tf_op jit(solution)/shard_map/all_gather | solution.py:116
  7.9 876.3 %all-gather.18.cloned.1.call-start = ((), (), s32[]{:S(2)}) async-start(), calls=%async_computation.5 | async-start | bytes 2359296 | tf_op jit(solution)/shard_map/all_gather | solution.py:119
  8.7 881.4 %all-gather.20.cloned.1.call-start = ((), (), s32[]{:S(2)}) async-start(), calls=%async_computation.6 | async-start | bytes 9437184 | tf_op jit(solution)/shard_map/all_gather | solution.py:124
  9.4 908.8 %all-gather.22.cloned.1.call-start = ((), (), s32[]{:S(2)}) async-start(), calls=%async_computation.7 | async-start | bytes 9437184 | tf_op jit(solution)/shard_map/all_gather | solution.py:126
  32.0 86.8 %copy-start.12 = (f32[8,1,128]{2,1,0:T(1,128)}, f32[8,1,128]{2,1,0:T(1,128)S(1)}, u32[]{:S(2)}) copy-start(f32[8,1,128]{2,1,0:T(1,128)S(1)} %convert_element_type.277) | copy-start | bytes 12292
  48.7 70.1 %copy-start.19 = (f32[8,1,128]{2,1,0:T(1,128)}, f32[8,1,128]{2,1,0:T(1,128)S(1)}, u32[]{:S(2)}) copy-start(f32[8,1,128]{2,1,0:T(1,128)S(1)} %convert_element_type.278) | copy-start | bytes 12292
  85.3 33.5 %copy-start.21 = (f32[512]{0:T(512)}, f32[512]{0:T(512)S(1)}, u32[]{:S(2)}) copy-start(f32[512]{0:T(512)S(1)} %broadcast_multiply_fusion.1) | copy-start | bytes 6148
  87.6 31.3 %copy-start.24 = (f32[512]{0:T(512)}, f32[512]{0:T(512)S(1)}, u32[]{:S(2)}) copy-start(f32[512]{0:T(512)S(1)} %fusion.83) | copy-start | bytes 6148
  120.5 13.4 copy-start.41
  120.5 16.2 copy-start.49
  120.5 157.4 %copy-start.50 = (bf16[128]{0:T(256)(128)(2,1)S(1)}, bf16[128]{0:T(256)(128)(2,1)}, u32[]{:S(2)}) copy-start(bf16[128]{0:T(256)(128)(2,1)} %param.31) | copy-start | bytes 772
  120.5 266.7 %copy-start.51 = (bf16[128]{0:T(256)(128)(2,1)S(1)}, bf16[128]{0:T(256)(128)(2,1)}, u32[]{:S(2)}) copy-start(bf16[128]{0:T(256)(128)(2,1)} %param.33) | copy-start | bytes 772
  120.5 283.1 %copy-start.48 = (bf16[512]{0:T(512)(128)(2,1)S(1)}, bf16[512]{0:T(512)(128)(2,1)}, u32[]{:S(2)}) copy-start(bf16[512]{0:T(512)(128)(2,1)} %param.36) | copy-start | bytes 3076
  120.5 309.6 %copy-start.52 = (bf16[128]{0:T(256)(128)(2,1)S(1)}, bf16[128]{0:T(256)(128)(2,1)}, u32[]{:S(2)}) copy-start(bf16[128]{0:T(256)(128)(2,1)} %param.34) | copy-start | bytes 772
  120.5 326.7 %copy-start.53 = (bf16[128]{0:T(256)(128)(2,1)S(1)}, bf16[128]{0:T(256)(128)(2,1)}, u32[]{:S(2)}) copy-start(bf16[128]{0:T(256)(128)(2,1)} %param.39) | copy-start | bytes 772
  122.0 361.9 %collective-permute-start = (bf16[512,2048]{1,0:T(8,128)(2,1)}, bf16[512,2048]{1,0:T(8,128)(2,1)S(1)}, u32[]{:S(2)}, u32[]{:S(2)}) collective-permute-start(bf16[512,2048]{1,0:T(8,128)(2,1)} %slice.69), channel_id=1, source_target_pairs={{0,3},{1,4},{2,5},{3,6},{4,7},{5,8},{6,9},{7,10},{8,11},{9,12},{10... | collective-permute-start | bytes 6291464 | tf_op jit(solution)/shard_map/ppermute | solution.py:18
  124.1 367.1 %collective-permute-start.1 = (bf16[512,2048]{1,0:T(8,128)(2,1)}, bf16[512,2048]{1,0:T(8,128)(2,1)}, u32[]{:S(2)}, u32[]{:S(2)}) collective-permute-start(bf16[512,2048]{1,0:T(8,128)(2,1)} %slice.69), channel_id=1, source_target_pairs={{0,2},{1,3},{2,4},{3,5},{4,6},{5,7},{6,8},{7,9},{8,10},{9,11},{10,... | collective-permute-start | bytes 6291464 | tf_op jit(solution)/shard_map/ppermute | solution.py:18
  129.4 363.8 %collective-permute-start.2 = (bf16[512,2048]{1,0:T(8,128)(2,1)}, bf16[512,2048]{1,0:T(8,128)(2,1)}, u32[]{:S(2)}, u32[]{:S(2)}) collective-permute-start(bf16[512,2048]{1,0:T(8,128)(2,1)} %slice.69), channel_id=1, source_target_pairs={{0,1},{1,2},{2,3},{3,4},{4,5},{5,6},{6,7},{7,8},{8,9},{9,10},{10,1... | collective-permute-start | bytes 6291464 | tf_op jit(solution)/shard_map/ppermute | solution.py:18
  133.9 331.5 %collective-permute-start.6 = (s32[512]{0:T(512)S(1)}, s32[512]{0:T(512)S(1)}, u32[]{:S(2)}, u32[]{:S(2)}) collective-permute-start(s32[512]{0:T(512)S(1)} %broadcast_add_fusion), channel_id=1, source_target_pairs={{0,3},{1,4},{2,5},{3,6},{4,7},{5,8},{6,9},{7,10},{8,11},{9,12},{10... | collective-permute-start | bytes 6152 | tf_op jit(solution)/shard_map/ppermute | solution.py:18
  135.2 332.9 %collective-permute-start.7 = (s32[512]{0:T(512)S(1)}, s32[512]{0:T(512)S(1)}, u32[]{:S(2)}, u32[]{:S(2)}) collective-permute-start(s32[512]{0:T(512)S(1)} %broadcast_add_fusion), channel_id=1, source_target_pairs={{0,2},{1,3},{2,4},{3,5},{4,6},{5,7},{6,8},{7,9},{8,10},{9,11},{10,... | collective-permute-start | bytes 6152 | tf_op jit(solution)/shard_map/ppermute | solution.py:18
  136.5 1598.9 %reduce-scatter.7.cloned.1.call-start = ((), (), s32[]{:S(2)}) async-start(), calls=%async_computation.9 | async-start | bytes 2359296 | tf_op jit(solution)/shard_map/reduce_scatter | solution.py:312
  387.2 498.0 %copy-start.42 = (f32[8,1,128]{2,1,0:T(1,128)}, f32[8,1,128]{2,1,0:T(1,128)S(1)}, u32[]{:S(2)}) copy-start(f32[8,1,128]{2,1,0:T(1,128)S(1)} %convert_element_type.281) | copy-start | bytes 12292
  403.6 538.1 %copy-start.32 = (f32[8,1,128]{2,1,0:T(1,128)}, f32[8,1,128]{2,1,0:T(1,128)S(1)}, u32[]{:S(2)}) copy-start(f32[8,1,128]{2,1,0:T(1,128)S(1)} %convert_element_type.283) | copy-start | bytes 12292
  447.2 442.9 %copy-start.44 = (f32[8,1,128]{2,1,0:T(1,128)}, f32[8,1,128]{2,1,0:T(1,128)S(1)}, u32[]{:S(2)}) copy-start(f32[8,1,128]{2,1,0:T(1,128)S(1)} %convert_element_type.284) | copy-start | bytes 12292
  465.4 4.1 collective-permute-start.8
  468.2 5.5 collective-permute-start.9
  469.5 5.7 collective-permute-start.10
  473.6 49.8 %collective-permute-start.3 = (bf16[512,2048]{1,0:T(8,128)(2,1)}, bf16[512,2048]{1,0:T(8,128)(2,1)}, u32[]{:S(2)}, u32[]{:S(2)}) collective-permute-start(bf16[512,2048]{1,0:T(8,128)(2,1)} %slice.69), channel_id=1, source_target_pairs={{1,0},{2,1},{3,2},{4,3},{5,4},{6,5},{7,6},{8,7},{9,8},{10,9},{11,1... | collective-permute-start | bytes 6291464 | tf_op jit(solution)/shard_map/ppermute | solution.py:18
  475.1 7.5 collective-permute-start.11
  482.6 162.3 %collective-permute-start.4 = (bf16[512,2048]{1,0:T(8,128)(2,1)}, bf16[512,2048]{1,0:T(8,128)(2,1)}, u32[]{:S(2)}, u32[]{:S(2)}) collective-permute-start(bf16[512,2048]{1,0:T(8,128)(2,1)} %slice.69), channel_id=1, source_target_pairs={{2,0},{3,1},{4,2},{5,3},{6,4},{7,5},{8,6},{9,7},{10,8},{11,9},{12,... | collective-permute-start | bytes 6291464 | tf_op jit(solution)/shard_map/ppermute | solution.py:18
  483.9 213.1 %collective-permute-start.5 = (bf16[512,2048]{1,0:T(8,128)(2,1)}, bf16[512,2048]{1,0:T(8,128)(2,1)}, u32[]{:S(2)}, u32[]{:S(2)}) collective-permute-start(bf16[512,2048]{1,0:T(8,128)(2,1)} %slice.69), channel_id=1, source_target_pairs={{3,0},{4,1},{5,2},{6,3},{7,4},{8,5},{9,6},{10,7},{11,8},{12,9},{13... | collective-permute-start | bytes 6291464 | tf_op jit(solution)/shard_map/ppermute | solution.py:18
  889.7 52.0 %copy-start.4 = (f32[512,1024]{1,0:T(8,128)}, f32[512,1024]{1,0:T(8,128)S(1)}, u32[]{:S(2)}) copy-start(f32[512,1024]{1,0:T(8,128)S(1)} %get-tuple-element.330) | copy-start | bytes 6291460
  889.7 52.0 %copy-start.28 = (f32[512]{0:T(512)}, f32[512]{0:T(512)S(1)}, u32[]{:S(2)}) copy-start(f32[512]{0:T(512)S(1)} %broadcast_multiply_fusion) | copy-start | bytes 6148
  890.1 51.6 %copy-start.38 = (f32[512]{0:T(512)}, f32[512]{0:T(512)S(1)}, u32[]{:S(2)}) copy-start(f32[512]{0:T(512)S(1)} %fusion.84) | copy-start | bytes 6148
  890.1 28.1 %copy-start.14 = (bf16[512,1024]{1,0:T(8,128)(2,1)S(1)}, bf16[512,1024]{1,0:T(8,128)(2,1)}, u32[]{:S(2)}) copy-start(bf16[512,1024]{1,0:T(8,128)(2,1)} %param.24) | copy-start | bytes 3145732
  890.2 28.1 %copy-start.30 = (f32[8,1,128]{2,1,0:T(1,128)S(1)}, f32[8,1,128]{2,1,0:T(1,128)}, u32[]{:S(2)}) copy-start(f32[8,1,128]{2,1,0:T(1,128)} %convert_element_type.282) | copy-start | bytes 12292
  918.2 15.5 copy-start.55
  1311.8 72.6 %copy-start.7 = (bf16[16,512,64]{1,2,0:T(8,128)(2,1)}, bf16[16,512,64]{1,2,0:T(8,128)(2,1)S(1)}, u32[]{:S(2)}) copy-start(bf16[16,512,64]{1,2,0:T(8,128)(2,1)S(1)} %get-tuple-element.123) | copy-start | bytes 3145732
  1311.8 11.7 copy-start.1
  1311.8 11.7 copy-start.13
  1311.8 11.7 copy-start.20
  1311.8 11.7 copy-start.22
  1311.9 11.7 copy-start.25
  1322.1 67.9 %collective-permute-start.12 = (bf16[512,2048]{0,1:T(8,128)(2,1)}, bf16[512,2048]{0,1:T(8,128)(2,1)}, u32[]{:S(2)}, u32[]{:S(2)}) collective-permute-start(bf16[512,2048]{0,1:T(8,128)(2,1)} %get-tuple-element.340), channel_id=1, source_target_pairs={{3,0},{4,1},{5,2},{6,3},{7,4},{8,5},{9,6},{10,7},{11,8},{12,9},{13... | collective-permute-start | bytes 6291464 | tf_op jit(solution)/shard_map/ppermute | solution.py:18
  1327.9 95.2 %collective-permute-start.13 = (bf16[512,2048]{0,1:T(8,128)(2,1)}, bf16[512,2048]{0,1:T(8,128)(2,1)}, u32[]{:S(2)}, u32[]{:S(2)}) collective-permute-start(bf16[512,2048]{0,1:T(8,128)(2,1)} %get-tuple-element.341), channel_id=1, source_target_pairs={{2,0},{3,1},{4,2},{5,3},{6,4},{7,5},{8,6},{9,7},{10,8},{11,9},{12,... | collective-permute-start | bytes 6291464 | tf_op jit(solution)/shard_map/ppermute | solution.py:18
  1330.7 132.9 %collective-permute-start.14 = (bf16[512,2048]{0,1:T(8,128)(2,1)}, bf16[512,2048]{0,1:T(8,128)(2,1)}, u32[]{:S(2)}, u32[]{:S(2)}) collective-permute-start(bf16[512,2048]{0,1:T(8,128)(2,1)} %get-tuple-element.342), channel_id=1, source_target_pairs={{1,0},{2,1},{3,2},{4,3},{5,4},{6,5},{7,6},{8,7},{9,8},{10,9},{11,1... | collective-permute-start | bytes 6291464 | tf_op jit(solution)/shard_map/ppermute | solution.py:18
  1333.5 170.1 %collective-permute-start.15 = (bf16[512,2048]{0,1:T(8,128)(2,1)}, bf16[512,2048]{0,1:T(8,128)(2,1)}, u32[]{:S(2)}, u32[]{:S(2)}) collective-permute-start(bf16[512,2048]{0,1:T(8,128)(2,1)} %get-tuple-element.343), channel_id=1, source_target_pairs={{0,1},{1,2},{2,3},{3,4},{4,5},{5,6},{6,7},{7,8},{8,9},{9,10},{10,1... | collective-permute-start | bytes 6291464 | tf_op jit(solution)/shard_map/ppermute | solution.py:18
  1379.8 127.0 %collective-permute-start.16 = (bf16[512,2048]{0,1:T(8,128)(2,1)}, bf16[512,2048]{0,1:T(8,128)(2,1)}, u32[]{:S(2)}, u32[]{:S(2)}) collective-permute-start(bf16[512,2048]{0,1:T(8,128)(2,1)} %get-tuple-element.344), channel_id=1, source_target_pairs={{0,2},{1,3},{2,4},{3,5},{4,6},{5,7},{6,8},{7,9},{8,10},{9,11},{10,... | collective-permute-start | bytes 6291464 | tf_op jit(solution)/shard_map/ppermute | solution.py:18
  1390.0 119.9 %collective-permute-start.17 = (bf16[512,2048]{0,1:T(8,128)(2,1)}, bf16[512,2048]{0,1:T(8,128)(2,1)}, u32[]{:S(2)}, u32[]{:S(2)}) collective-permute-start(bf16[512,2048]{0,1:T(8,128)(2,1)} %get-tuple-element.339), channel_id=1, source_target_pairs={{0,3},{1,4},{2,5},{3,6},{4,7},{5,8},{6,9},{7,10},{8,11},{9,12},{10... | collective-permute-start | bytes 6291464 | tf_op jit(solution)/shard_map/ppermute | solution.py:18
  1400.6 404.3 %reduce-scatter.5.cloned.1.call-start = ((), (), s32[]{:S(2)}) async-start(), calls=%async_computation.8 | async-start | bytes 7077888 | tf_op jit(solution)/shard_map/reduce_scatter | solution.py:303
  1539.1 417.6 %reduce-scatter.9.cloned.1.call-start = ((), (), s32[]{:S(2)}) async-start(), calls=%async_computation.10 | async-start | bytes 9437184 | tf_op jit(solution)/shard_map/reduce_scatter | solution.py:327
  1549.9 558.9 %reduce-scatter.11.cloned.1.call-start = ((), (), s32[]{:S(2)}) async-start(), calls=%async_computation.11 | async-start | bytes 9437184 | tf_op jit(solution)/shard_map/reduce_scatter | solution.py:333
  1560.0 128.4 %copy-start.57 = (u32[32]{0:T(128)S(1)}, u32[32]{0:T(128)}, u32[]{:S(2)}) copy-start(u32[32]{0:T(128)} %constant.142) | copy-start | bytes 388
  1560.1 131.8 %copy-start.8 = (bf16[16,512,64]{1,2,0:T(8,128)(2,1)S(1)}, bf16[16,512,64]{1,2,0:T(8,128)(2,1)}, u32[]{:S(2)}) copy-start(bf16[16,512,64]{1,2,0:T(8,128)(2,1)} %copy-done.7) | copy-start | bytes 3145732
  1560.1 619.6 %all-reduce.16.cloned.1.call-start = ((), (), s32[]{:S(2)}) async-start(), calls=%async_computation.12 | async-start | bytes 6291456 | tf_op jit(solution)/shard_map/psum | solution.py:346
  1723.7 6.9 copy-start.27
  1731.7 377.1 %copy-start.37 = (f32[512]{0:T(512)S(1)}, f32[512]{0:T(512)}, u32[]{:S(2)}) copy-start(f32[512]{0:T(512)} %copy-done.36) | copy-start | bytes 6148
  1731.7 377.1 %copy-start.43 = (f32[8,1,128]{2,1,0:T(1,128)S(1)}, f32[8,1,128]{2,1,0:T(1,128)}, u32[]{:S(2)}) copy-start(f32[8,1,128]{2,1,0:T(1,128)} %copy-done.42) | copy-start | bytes 12292
  2108.8 13.7 copy-start.34
  2108.8 13.7 copy-start.35
  2108.8 13.7 copy-start.40
  2108.9 13.7 copy-start.46
  2108.9 13.7 copy-start.47
  (51 other events, 164.3 us)
Sparse Core Ops, SparseCore 0:
  10.2 101.8 all-gather.15
  114.2 186.0 all-gather.17
  302.5 139.8 all-gather.19
  444.4 219.3 all-gather.21
  1400.7 283.5 reduce-scatter.6
  1687.8 117.0 reduce-scatter.4
  1808.5 148.1 reduce-scatter.8
  1960.8 147.9 reduce-scatter.10
  2111.4 68.2 all-reduce.15
where the time goes:
time: 2210 us; the launch traced here: 2190 us
  waiting for transfers between devices  702 us (32%)
  blocking collectives  572 us (26%)
  matrix products  559 us (25%)
  other arithmetic  155 us (7%)
  local copies, waits for them, and re-layouts  103 us (5%)
  starting transfers between devices  86 us (4%)
    ppermute x18, waiting for transfers between devices, passed_along(): lax.ppermute(value, axis, [(source, source + steps) for source in range(l...  293 us
    dot_general x54, matrix products, dot_second_t(): lax.dot_general(first_op, second_op, (((1,), (1,)), ((), ())), preferred_...  289 us
    reduce_scatter x1, waiting for transfers between devices, local(): lax.psum_scatter(output_weight_grad.astype(jnp.bfloat16), 'fsdp', scatter...  152 us
    reduce_scatter x1, waiting for transfers between devices, local(): lax.psum_scatter(hidden_weight_grad.astype(jnp.bfloat16), 'fsdp', scatter...  152 us
    all_gather x1, blocking collectives, local(): lax.all_gather(attn_scale, 'fsdp', axis=0, tiled=True)  141 us
    dot_general x36, matrix products, plain_dot(): return jnp.dot(first_op, second_op, preferred_element_type=jnp.float32)  137 us
    dot_general x38, matrix products, dot_first_t(): lax.dot_general(first_op, second_op, (((0,), (0,)), ((), ())), preferred_...  132 us
    all_gather x1, blocking collectives, local(): lax.all_gather(output_bias, 'fsdp', axis=0, tiled=True)  128 us
  transfers between devices with their start and end apart: 27, of which 14 were waited for; matrix products, arithmetic and copies ran while one was open for 18% of the time, Pallas kernels for 0%

commit v1 on v0

v1 whole, which is shorter than its diff:
```python
import jax
import jax.numpy as jnp
from jax import lax
from jax.experimental import pallas as pl
from jax.experimental.pallas import tpu as pltpu
from jax.sharding import PartitionSpec as P

H = 16
HD = 64
REACH = 3
EPS = 1e-06
NEG = -1e30
LOG2E = 1.4426950408889634
Q_TILE = 256
K_TILE_FWD = 512
K_TILE_BWD = 256


def passed_along(value, axis, steps):
    count = lax.axis_size(axis)
    leading, last = (max(0, -steps), min(count, count - steps))
    return lax.ppermute(value, axis, [(source, source + steps) for source in range(leading, last)])


def layer_norm_parts(matrix):
    average = jnp.mean(matrix, axis=-1, keepdims=True)
    centred = matrix - average
    second_moment = jnp.mean(centred * centred, axis=-1, keepdims=True)
    inverse = lax.rsqrt(second_moment + EPS)
    return centred * inverse, inverse


def layer_norm_back(grad, normed, inverse):
    first = jnp.mean(grad, axis=-1, keepdims=True)
    second = jnp.mean(grad * normed, axis=-1, keepdims=True)
    return (grad - first - normed * second) * inverse


def plain_dot(first_op, second_op):
    return jnp.dot(first_op, second_op, preferred_element_type=jnp.float32)


def dot_first_t(first_op, second_op):
    return lax.dot_general(
        first_op, second_op, (((0,), (0,)), ((), ())), preferred_element_type=jnp.float32
    )


def dot_second_t(first_op, second_op):
    return lax.dot_general(
        first_op, second_op, (((1,), (1,)), ((), ())), preferred_element_type=jnp.float32
    )


def column_sum(matrix):
    return jnp.sum(matrix.astype(jnp.float32), axis=0)


def as_float(vector):
    return vector.astype(jnp.float32)


def two_heads(block):
    low_half = lax.broadcasted_iota(jnp.int32, block.shape, 1) < HD
    zero = jnp.zeros_like(block)
    return jnp.concatenate([jnp.where(low_half, block, zero), jnp.where(low_half, zero, block)], axis=0)


def twice(row):
    return jnp.concatenate([row, row], axis=1)


def attend_kernel(limits, q_ref, kv_ref, cq_ref, ck_ref, o_ref, lse_ref):
    rows = q_ref.shape[0]
    step = K_TILE_FWD
    per_block = rows // step
    for tile in range(rows // Q_TILE):
        here = pl.ds(tile * Q_TILE, Q_TILE)
        q_pair = two_heads(q_ref[here, :])
        codes = twice(cq_ref[:, here])

        def body(index, carry):
            peak, total, acc = carry
            block = index // per_block
            place = pl.ds((index % per_block) * step, step)
            keys = kv_ref[block, 0, place, :]
            values_t = kv_ref[block, 1, place, :].T
            same = ck_ref[pl.ds(pl.multiple_of(index * step, step), step), :] == codes
            scores = dot_second_t(keys, q_pair) * (HD ** (-0.5) * LOG2E)
            scores = jnp.where(same, scores, NEG)
            new_peak = jnp.maximum(peak, jnp.max(scores, axis=0, keepdims=True))
            weights = jnp.exp2(scores - new_peak)
            decay = jnp.exp2(peak - new_peak)
            total = total * decay + jnp.sum(weights, axis=0, keepdims=True)
            low = weights.astype(jnp.bfloat16)
            part = jnp.concatenate(
                [
                    plain_dot(values_t[:HD, :], low[:, :Q_TILE]),
                    plain_dot(values_t[HD:, :], low[:, Q_TILE:]),
                ],
                axis=1,
            )
            return new_peak, total, acc * decay + part

        start = (
            jnp.full((1, 2 * Q_TILE), NEG, jnp.float32),
            jnp.zeros((1, 2 * Q_TILE), jnp.float32),
            jnp.zeros((HD, 2 * Q_TILE), jnp.float32),
        )
        first = limits[2 * tile] // (step // K_TILE_BWD)
        last = (limits[2 * tile + 1] + step // K_TILE_BWD - 1) // (step // K_TILE_BWD)
        peak, total, acc = lax.fori_loop(first, last, body, start)
        acc = acc / total
        o_ref[here, :] = jnp.concatenate([acc[:, :Q_TILE], acc[:, Q_TILE:]], axis=0).T
        lse_ref[0, :, pl.ds(tile * 2 * Q_TILE, 2 * Q_TILE)] = peak + jnp.log(total) * LOG2E


def attend_back_kernel(
    limits, q_ref, kv_ref, go_ref, o_ref, lse_ref, cq_ref, ck_ref, dq_ref, dkv_ref, acc_ref
):
    rows = q_ref.shape[0]
    step = K_TILE_BWD
    per_block = rows // step
    score_scale = HD ** (-0.5)
    acc_ref[...] = jnp.zeros_like(acc_ref)
    for tile in range(rows // Q_TILE):
        here = pl.ds(tile * Q_TILE, Q_TILE)
        q_pair = two_heads(q_ref[here, :])
        go = go_ref[here, :]
        go_pair = two_heads(go)
        inner = (go.astype(jnp.float32) * o_ref[here, :]).T
        inner = jnp.concatenate(
            [
                jnp.sum(inner[:HD, :], axis=0, keepdims=True),
                jnp.sum(inner[HD:, :], axis=0, keepdims=True),
            ],
            axis=1,
        )
        lse = lse_ref[0, :, pl.ds(tile * 2 * Q_TILE, 2 * Q_TILE)]
        codes = twice(cq_ref[:, here])

        def body(index, dq):
            block = index // per_block
            place = pl.ds((index % per_block) * step, step)
            keys = kv_ref[block, 0, place, :]
            values = kv_ref[block, 1, place, :]
            keys_t = keys.T
            same = ck_ref[pl.ds(pl.multiple_of(index * step, step), step), :] == codes
            scores = dot_second_t(keys, q_pair) * (score_scale * LOG2E)
            weights = jnp.where(same, jnp.exp2(scores - lse), 0.0)
            g_weights = dot_second_t(values, go_pair)
            g_scores = (weights * (g_weights - inner)).astype(jnp.bfloat16)
            acc_ref[block, 1, place, :] += plain_dot(weights.astype(jnp.bfloat16), go_pair)
            acc_ref[block, 0, place, :] += plain_dot(g_scores, q_pair)
            part = jnp.concatenate(
                [
                    plain_dot(keys_t[:HD, :], g_scores[:, :Q_TILE]),
                    plain_dot(keys_t[HD:, :], g_scores[:, Q_TILE:]),
                ],
                axis=0,
            )
            return dq + part

        dq = lax.fori_loop(
            limits[2 * tile],
            limits[2 * tile + 1],
            body,
            jnp.zeros((2 * HD, Q_TILE), jnp.float32),
        )
        dq_ref[here, :] = (dq * score_scale).T.astype(jnp.bfloat16)
    dkv_ref[:, 0, :, :] = (acc_ref[:, 0, :, :] * score_scale).astype(jnp.bfloat16)
    dkv_ref[:, 1, :, :] = acc_ref[:, 1, :, :].astype(jnp.bfloat16)


def attend(limits, queries, near, own_codes, near_codes):
    rows, width = queries.shape
    blocks = near.shape[0]
    pairs = width // (2 * HD)
    lanes = 2 * HD
    column = pl.BlockSpec((rows, lanes), lambda p, lim: (0, p))
    return pl.pallas_call(
        attend_kernel,
        grid_spec=pltpu.PrefetchScalarGridSpec(
            num_scalar_prefetch=1,
            grid=(pairs,),
            in_specs=[
                column,
                pl.BlockSpec((blocks, 2, rows, lanes), lambda p, lim: (0, 0, 0, p)),
                pl.BlockSpec((1, rows), lambda p, lim: (0, 0)),
                pl.BlockSpec((blocks * rows, 1), lambda p, lim: (0, 0)),
            ],
            out_specs=[column, pl.BlockSpec((1, 1, 2 * rows), lambda p, lim: (p, 0, 0))],
        ),
        out_shape=[
            jax.ShapeDtypeStruct((rows, width), jnp.float32),
            jax.ShapeDtypeStruct((pairs, 1, 2 * rows), jnp.float32),
        ],
        compiler_params=pltpu.CompilerParams(vmem_limit_bytes=48 * 2**20),
        cost_estimate=pl.CostEstimate(
            flops=16 * rows * rows * blocks * width // 2,
            bytes_accessed=2 * blocks * 2 * rows * width,
            transcendentals=0,
        ),
    )(limits, queries, near, own_codes[None, :], near_codes[:, None])


def attend_back(limits, queries, near, g_out, out, lse, own_codes, near_codes):
    rows, width = queries.shape
    blocks = near.shape[0]
    pairs = width // (2 * HD)
    lanes = 2 * HD
    column = pl.BlockSpec((rows, lanes), lambda p, lim: (0, p))
    window = pl.BlockSpec((blocks, 2, rows, lanes), lambda p, lim: (0, 0, 0, p))
    return pl.pallas_call(
        attend_back_kernel,
        grid_spec=pltpu.PrefetchScalarGridSpec(
            num_scalar_prefetch=1,
            grid=(pairs,),
            in_specs=[
                column,
                window,
                column,
                column,
                pl.BlockSpec((1, 1, 2 * rows), lambda p, lim: (p, 0, 0)),
                pl.BlockSpec((1, rows), lambda p, lim: (0, 0)),
                pl.BlockSpec((blocks * rows, 1), lambda p, lim: (0, 0)),
            ],
            out_specs=[column, window],
            scratch_shapes=[pltpu.VMEM((blocks, 2, rows, lanes), jnp.float32)],
        ),
        out_shape=[
            jax.ShapeDtypeStruct((rows, width), jnp.bfloat16),
            jax.ShapeDtypeStruct((blocks, 2, rows, width), jnp.bfloat16),
        ],
        compiler_params=pltpu.CompilerParams(vmem_limit_bytes=48 * 2**20),
        cost_estimate=pl.CostEstimate(
            flops=40 * rows * rows * blocks * width // 2,
            bytes_accessed=4 * blocks * 2 * rows * width,
            transcendentals=0,
        ),
    )(limits, queries, near, g_out, out, lse, own_codes[None, :], near_codes[:, None])


def tile_limits(own_codes, near_codes):
    same = own_codes[:, None] == near_codes[None, :]
    queries = own_codes.shape[0] // Q_TILE
    count = near_codes.shape[0] // K_TILE_BWD
    touched = jnp.any(same.reshape(queries, Q_TILE, count, K_TILE_BWD), axis=(1, 3))
    number = jnp.arange(count, dtype=jnp.int32)[None, :]
    first = jnp.min(jnp.where(touched, number, count), axis=1)
    last = jnp.max(jnp.where(touched, number + 1, 0), axis=1)
    return jnp.stack([first, last], axis=1).reshape(-1)


def side_offsets():
    return [offset for offset in range(-REACH, REACH + 1) if offset != 0]


def gathered_rows(weight):
    return lax.all_gather(weight, "fsdp", axis=0, tiled=True)


def reduced_rows(grad):
    part = lax.psum_scatter(grad.astype(jnp.bfloat16), "fsdp", scatter_dimension=0, tiled=True)
    return lax.psum(part, "rep").astype(jnp.float32)


def local(
    tokens,
    segment,
    cotangent,
    attn_norm_gain,
    attn_norm_bias,
    qkv_weight,
    query_bias,
    value_bias,
    proj_weight,
    proj_bias,
    attn_scale,
    mlp_norm_gain,
    mlp_norm_bias,
    hidden_weight,
    hidden_bias,
    output_weight,
    output_bias,
    mlp_scale,
):
    both = ("rep", "fsdp")
    fsdp = lax.axis_size("fsdp")
    model_width = tokens.shape[1]
    tok_rows = tokens.shape[0]
    offsets = side_offsets()

    place = lax.axis_index(both) * tok_rows + lax.iota(jnp.int32, tok_rows)
    own_codes = jnp.where(segment >= 0, segment + 1, -1 - place)
    side_codes = {offset: passed_along(own_codes, both, -offset) for offset in offsets}
    side_codes[0] = own_codes
    near_codes = jnp.concatenate([side_codes[o] for o in range(-REACH, REACH + 1)])
    limits = tile_limits(own_codes, near_codes)

    vectors = (
        attn_norm_gain,
        attn_norm_bias,
        query_bias,
        value_bias,
        proj_bias,
        attn_scale,
        mlp_norm_gain,
        mlp_norm_bias,
        output_bias,
        mlp_scale,
        hidden_bias,
    )
    packed_vectors = as_float(lax.all_gather(jnp.concatenate(vectors), "fsdp", axis=0))
    whole = []
    at = 0
    for vector in vectors:
        size = vector.shape[0]
        whole.append(packed_vectors[:, at : at + size].reshape(-1))
        at += size
    (
        gain_one,
        shift_one,
        bias_query,
        bias_value,
        bias_proj,
        scale_one,
        gain_two,
        shift_two,
        bias_output,
        scale_two,
        bias_hidden,
    ) = whole
    w_qkv = gathered_rows(qkv_weight)
    w_proj = gathered_rows(proj_weight)
    w_hidden = gathered_rows(hidden_weight)
    w_output = gathered_rows(output_weight)

    inputs = as_float(tokens)
    normed_one, inverse_one = layer_norm_parts(inputs)
    first_in = (normed_one * gain_one + shift_one).astype(jnp.bfloat16)
    kv_plain = plain_dot(first_in, w_qkv[:, model_width:])
    packed = jnp.stack(
        [kv_plain[:, :model_width], kv_plain[:, model_width:] + bias_value]
    ).astype(jnp.bfloat16)
    sides = {offset: passed_along(packed, both, -offset) for offset in offsets}
    sides[0] = packed
    queries = (plain_dot(first_in, w_qkv[:, :model_width]) + bias_query).astype(jnp.bfloat16)
    near = jnp.stack([sides[o] for o in range(-REACH, REACH + 1)])

    attended_wide, lse = attend(limits, queries, near, own_codes, near_codes)
    attended = attended_wide.astype(jnp.bfloat16)
    branch_one = plain_dot(attended, w_proj) + bias_proj
    middle = inputs + scale_one * branch_one
    normed_two, inverse_two = layer_norm_parts(middle)
    second_in = (normed_two * gain_two + shift_two).astype(jnp.bfloat16)
    hidden = plain_dot(second_in, w_hidden) + bias_hidden
    cdf = 0.5 * (1.0 + lax.erf(hidden * (0.5**0.5)))
    density = jnp.exp(-0.5 * hidden * hidden) * 0.3989422804014327
    active, slope = lax.optimization_barrier(
        ((hidden * cdf).astype(jnp.bfloat16), (cdf + hidden * density).astype(jnp.bfloat16))
    )
    branch_two = plain_dot(active, w_output) + bias_output
    block_output = (middle + scale_two * branch_two).astype(jnp.bfloat16)

    upstream = as_float(cotangent)
    scale_two_grad = jnp.sum(upstream * branch_two, axis=0)
    g_branch_two = (scale_two * upstream).astype(jnp.bfloat16)
    output_weight_grad = dot_first_t(active, g_branch_two).astype(jnp.bfloat16)
    output_bias_grad = column_sum(g_branch_two)
    g_hidden = (dot_second_t(g_branch_two, w_output) * as_float(slope)).astype(jnp.bfloat16)
    g_hidden, output_weight_grad = lax.optimization_barrier((g_hidden, output_weight_grad))
    hidden_weight_grad = dot_first_t(second_in, g_hidden).astype(jnp.bfloat16)
    hidden_bias_grad = column_sum(g_hidden)
    g_second = dot_second_t(g_hidden, w_hidden)
    gain_two_grad = jnp.sum(g_second * normed_two, axis=0)
    shift_two_grad = jnp.sum(g_second, axis=0)
    g_middle = upstream + layer_norm_back(g_second * gain_two, normed_two, inverse_two)
    scale_one_grad = jnp.sum(g_middle * branch_one, axis=0)
    g_branch_one = (scale_one * g_middle).astype(jnp.bfloat16)
    proj_weight_grad = dot_first_t(attended, g_branch_one).astype(jnp.bfloat16)
    proj_bias_grad = column_sum(g_branch_one)
    g_attended = dot_second_t(g_branch_one, w_proj).astype(jnp.bfloat16)
    g_attended, hidden_weight_grad, proj_weight_grad = lax.optimization_barrier(
        (g_attended, hidden_weight_grad, proj_weight_grad)
    )
    output_weight_out = reduced_rows(output_weight_grad)
    hidden_weight_out = reduced_rows(hidden_weight_grad)
    proj_weight_out = reduced_rows(proj_weight_grad)

    g_query, g_near = attend_back(
        limits, queries, near, g_attended, attended_wide, lse, own_codes, near_codes
    )
    arrived = [passed_along(g_near[offset + REACH], both, offset) for offset in offsets]
    query_weight_grad = dot_first_t(first_in, g_query).astype(jnp.bfloat16)
    query_bias_grad = column_sum(g_query)
    g_first = dot_second_t(g_query, w_qkv[:, :model_width])
    g_kv = as_float(g_near[REACH])
    for piece in arrived:
        g_kv = g_kv + as_float(piece)
    value_bias_grad = jnp.sum(g_kv[1], axis=0)
    g_keys, g_values = g_kv[0].astype(jnp.bfloat16), g_kv[1].astype(jnp.bfloat16)
    g_kv_low = jnp.concatenate([g_keys, g_values], axis=1)
    kv_weight_grad = dot_first_t(first_in, g_kv_low).astype(jnp.bfloat16)
    g_first = g_first + dot_second_t(g_kv_low, w_qkv[:, model_width:])
    qkv_weight_out = jnp.concatenate(
        [reduced_rows(query_weight_grad), reduced_rows(kv_weight_grad)], axis=1
    )
    gain_one_grad = jnp.sum(g_first * normed_one, axis=0)
    shift_one_grad = jnp.sum(g_first, axis=0)
    input_grad = g_middle + layer_norm_back(g_first * gain_one, normed_one, inverse_one)

    small = (
        gain_one_grad,
        shift_one_grad,
        query_bias_grad,
        value_bias_grad,
        proj_bias_grad,
        scale_one_grad,
        gain_two_grad,
        shift_two_grad,
        output_bias_grad,
        scale_two_grad,
        hidden_bias_grad,
    )
    small_rows = jnp.concatenate([vector.reshape(fsdp, -1) for vector in small], axis=1)
    small_sum = lax.psum(
        lax.psum_scatter(small_rows, "fsdp", scatter_dimension=0, tiled=True), "rep"
    ).reshape(-1)
    owned = []
    at = 0
    for vector in small:
        size = vector.shape[0] // fsdp
        owned.append(small_sum[at : at + size])
        at += size
    return (
        block_output,
        input_grad,
        owned[0],
        owned[1],
        qkv_weight_out,
        owned[2],
        owned[3],
        proj_weight_out,
        owned[4],
        owned[5],
        owned[6],
        owned[7],
        hidden_weight_out,
        owned[10],
        output_weight_out,
        owned[8],
        owned[9],
    )


def solution(mesh):
    return jax.shard_map(
        local,
        mesh=mesh,
        in_specs=(
            P(("rep", "fsdp"), None),
            P(("rep", "fsdp")),
            P(("rep", "fsdp"), None),
            P("fsdp"),
            P("fsdp"),
            P("fsdp", None),
            P("fsdp"),
            P("fsdp"),
            P("fsdp", None),
            P("fsdp"),
            P("fsdp"),
            P("fsdp"),
            P("fsdp"),
            P("fsdp", None),
            P("fsdp"),
            P("fsdp", None),
            P("fsdp"),
            P("fsdp"),
        ),
        out_specs=(
            P(("rep", "fsdp"), None),
            P(("rep", "fsdp"), None),
            P("fsdp"),
            P("fsdp"),
            P("fsdp", None),
            P("fsdp"),
            P("fsdp"),
            P("fsdp", None),
            P("fsdp"),
            P("fsdp"),
            P("fsdp"),
            P("fsdp"),
            P("fsdp", None),
            P("fsdp"),
            P("fsdp", None),
            P("fsdp"),
            P("fsdp"),
        ),
        check_vma=False,
    )
```

time: 2210 us -> 1710 us (0.77)
  waiting for transfers between devices: 702 us -> 1200 us
  blocking collectives: 572 us -> 74.2 us
  matrix products: 559 us -> 92.6 us
  other arithmetic: 155 us -> 29.7 us
  Pallas kernels: 0 us -> 92.6 us
  starting transfers between devices: 86 us -> 151 us
  local copies, waits for them, and re-layouts: 103 us -> 39.3 us
    all_gather x11 -> x1, blocking collectives: 530 us -> 32.8 us  [local(): lax.all_gather(jnp.concatenate(vectors), 'fsdp', axis=0)]
    ppermute x18, waiting for transfers between devices: 293 us -> 556 us  [passed_along(): lax.ppermute(value, axis, [(source, source + steps) for source in range(l...]
    dot_general x54 -> x5, matrix products: 289 us -> 32.5 us  [dot_second_t(): lax.dot_general(first_op, second_op, (((1,), (1,)), ((), ())), preferred_...]
    all_gather x4, waiting for transfers between devices: 24.6 us -> 179 us  [gathered_rows(): return lax.all_gather(weight, 'fsdp', axis=0, tiled=True)]
    dot_general x38 -> x5, matrix products: 132 us -> 24.7 us  [dot_first_t(): lax.dot_general(first_op, second_op, (((0,), (0,)), ((), ())), preferred_...]
    dot_general x36 -> x5, matrix products: 137 us -> 35.4 us  [plain_dot(): return jnp.dot(first_op, second_op, preferred_element_type=jnp.float32)]
    pallas_call x0 -> x2, Pallas kernels: none -> 92.6 us  [the longest x1 56.6 us: attend_back(): pl.pallas_call(attend_back_kernel, grid_spec=pltpu.PrefetchScalarGridSpec...]
    convert_element_type x43 -> x3, other arithmetic: 92.7 us -> 6.2 us  [reduced_rows(): return lax.psum(part, 'rep').astype(jnp.float32)]
  transfers between devices with their start and end apart: 27 -> 28, of which waited for: 14 -> 16; matrix products, arithmetic and copies ran while one was open for 18% -> 5% of each run, Pallas kernels for 0% -> 2%
where the time goes in v1:
time: 1710 us; the launch traced here: 1700 us
  waiting for transfers between devices  1200 us (70%)
  starting transfers between devices  151 us (9%)
  matrix products  92.6 us (5%)
  Pallas kernels  92.6 us (5%)
  blocking collectives  74.2 us (4%)
  local copies, waits for them, and re-layouts  39.3 us (2%)
  other arithmetic  29.7 us (2%)
    ppermute x18, waiting for transfers between devices, passed_along(): lax.ppermute(value, axis, [(source, source + steps) for source in range(l...  556 us
    reduce_scatter x5, waiting for transfers between devices, reduced_rows(): lax.psum_scatter(grad.astype(jnp.bfloat16), 'fsdp', scatter_dimension=0,...  443 us
    all_gather x4, waiting for transfers between devices, gathered_rows(): return lax.all_gather(weight, 'fsdp', axis=0, tiled=True)  179 us
    ppermute x18, starting transfers between devices, passed_along(): lax.ppermute(value, axis, [(source, source + steps) for source in range(l...  150 us
    pallas_call x1, Pallas kernels, attend_back(): pl.pallas_call(attend_back_kernel, grid_spec=pltpu.PrefetchScalarGridSpec...  56.6 us
    pallas_call x1, Pallas kernels, attend(): pl.pallas_call(attend_kernel, grid_spec=pltpu.PrefetchScalarGridSpec(num_...  36 us
    unnamed x1, blocking collectives  35.6 us
    dot_general x5, matrix products, plain_dot(): return jnp.dot(first_op, second_op, preferred_element_type=jnp.float32)  35.4 us
  transfers between devices with their start and end apart: 28, of which 16 were waited for; matrix products, arithmetic and copies ran while one was open for 5% of the time, Pallas kernels for 2%

profile of v1, /device:TPU:0, one launch (start us, length us, event | category | flops | bytes accessed | tf_op | source)
XLA Modules:
  0.0 1699.1 jit_solution(13110920606987473215)
XLA Ops:
  12.6 32.8 %all-gather.1 = bf16[8,1,1792]{2,1,0:T(2,128)(2,1)S(1)} all-gather(bf16[1,1,1792]{2,1,0:T(2,128)(2,1)S(1)} %reshape.210), channel_id=2, replica_groups=mesh['rep'=4,'fsdp'=8] {'fsdp'}, dimensions={0}, use_global_device_ids=true | all-gather | bytes 32256 | tf_op jit(solution)/shard_map/all_gather | solution.py:314
  46.1 66.4 %all-gather.7.cloned.1.call-done = bf16[1024,3072]{1,0:T(8,128)(2,1)} async-done(((bf16[128,3072]{1,0:T(8,128)(2,1)}), bf16[1024,3072]{1,0:T(8,128)(2,1)}) %all-gather.7.cloned.1.call-update) | async-done | bytes 6291472 | tf_op jit(solution)/shard_map/all_gather | solution.py:260
  112.5 4.6 fusion.12
  120.1 3.3 collective-permute-start.6
  123.4 3.4 collective-permute-start
  126.8 2.3 collective-permute-start.1
  129.2 3.4 collective-permute-start.2
  133.9 41.1 %collective-permute-done = s32[512]{0:T(512)S(1)} collective-permute-done((s32[512]{0:T(512)S(1)}, s32[512]{0:T(512)S(1)}, u32[]{:S(2)}, u32[]{:S(2)}) %collective-permute-start) | collective-permute-done | bytes 2080 | tf_op jit(solution)/shard_map/ppermute | solution.py:22
  175.0 4.9 collective-permute-start.7
  182.5 65.3 %collective-permute-start.8 = (bf16[2,512,1024]{2,1,0:T(8,128)(2,1)}, bf16[2,512,1024]{2,1,0:T(8,128)(2,1)}, u32[]{:S(2)}, u32[]{:S(2)}) collective-permute-start(bf16[2,512,1024]{2,1,0:T(8,128)(2,1)} %pad_maximum_fusion), channel_id=1, source_target_pairs={{0,1},{1,2},{2,3},{3,4},{4,5},{5,6},{6,7},{7,8},{8,9},{9,10},{10,1... | collective-permute-start | bytes 6291464 | tf_op jit(solution)/shard_map/ppermute | solution.py:22
  247.8 77.2 %collective-permute-done.5 = s32[512]{0:T(512)S(1)} collective-permute-done((s32[512]{0:T(512)S(1)}, s32[512]{0:T(512)S(1)}, u32[]{:S(2)}, u32[]{:S(2)}) %collective-permute-start.5) | collective-permute-done | bytes 2080 | tf_op jit(solution)/shard_map/ppermute | solution.py:22
  329.7 1.5 collective-permute-start.11
  331.3 2.9 add_convert_fusion.2.q_ref
  334.2 1.8 bitcast_dynamic-update-slice_fusion.5
  335.9 1.8 bitcast_dynamic-update-slice_fusion.4
  337.7 1.8 bitcast_dynamic-update-slice_fusion.3
  339.8 113.4 %collective-permute-done.9 = bf16[2,512,1024]{2,1,0:T(8,128)(2,1)} collective-permute-done((bf16[2,512,1024]{2,1,0:T(8,128)(2,1)}, bf16[2,512,1024]{2,1,0:T(8,128)(2,1)}, u32[]{:S(2)}, u32[]{:S(2)}) %collective-permute-start.9) | collective-permute-done | bytes 2097184 | tf_op jit(solution)/shard_map/ppermute | solution.py:22
  453.2 1.8 bitcast_dynamic-update-slice_fusion.2
  455.0 72.3 %collective-permute-done.10 = bf16[2,512,1024]{2,1,0:T(8,128)(2,1)} collective-permute-done((bf16[2,512,1024]{2,1,0:T(8,128)(2,1)}, bf16[2,512,1024]{2,1,0:T(8,128)(2,1)}, u32[]{:S(2)}, u32[]{:S(2)}) %collective-permute-start.10) | collective-permute-done | bytes 2097184 | tf_op jit(solution)/shard_map/ppermute | solution.py:22
  527.3 1.8 bitcast_dynamic-update-slice_fusion.1
  529.1 7.6 collective-permute-done.11
  536.8 5.2 copy-done.18
  542.0 36.0 %shard_map.305 = (f32[512,1024]{1,0:T(8,128)S(1)}, f32[8,1,1024]{2,1,0:T(1,128)S(1)}) custom-call(s32[4]{0:T(128)S(1)} %reshape.195.limits, bf16[512,1024]{1,0:T(8,128)(2,1)S(1)} %add_convert_fusion.2.q_ref, bf16[7,2,512,1024]{3,2,1,0:T(8,128)(2,1)} %copy-done.18, s32[1,512]{1,0:T(1,128)S(1)} %bitcast.124, s32[3584,1]{1,0:T(8,128)S(1)} %broadcast_in_dim.45.ck_ref), custom_call_target="tpu_custom_call" | custom-call | flops 15032385536 | bytes 14680064 | tf_op jit(solution)/shard_map/pallas_call | solution.py:181
  578.1 5.2 fusion.58
  585.1 12.0 fusion.4
  597.1 2.0 copy-done.35
  599.1 7.5 convolution_convert_fusion.1
  606.6 112.5 %all-gather.13.cloned.1.call-done = bf16[4096,1024]{1,0:T(8,128)(2,1)} async-done(((bf16[512,1024]{1,0:T(8,128)(2,1)}), bf16[4096,1024]{1,0:T(8,128)(2,1)}) %all-gather.13.cloned.1.call-update) | async-done | bytes 8388624 | tf_op jit(solution)/shard_map/all_gather | solution.py:260
  719.1 9.6 multiply_convert_fusion
  728.7 2.1 copy-done.10
  730.8 7.2 convolution_convert_fusion
  738.1 10.3 multiply_reduce_fusion
  748.5 10.6 fusion.29
  759.0 1.9 convert_reduce_fusion.3
  761.9 2.6 convolution_convert_fusion.4
  764.6 3.3 convolution_convert_fusion.5.go_ref
  767.9 56.6 %shard_map.306 = (bf16[512,1024]{1,0:T(8,128)(2,1)S(1)}, bf16[7,2,512,1024]{3,2,1,0:T(8,128)(2,1)}) custom-call(s32[4]{0:T(128)S(1)} %reshape.195.limits, bf16[512,1024]{1,0:T(8,128)(2,1)S(1)} %add_convert_fusion.2.q_ref, bf16[7,2,512,1024]{3,2,1,0:T(8,128)(2,1)} %copy-done.18, bf16[512,1024]{1,0:T(8,128)(2,1)S(1)} %convolution_convert_fusion.5.go_ref, ...), custom_call_target="tpu_custom_call" | custom-call | flops 37580963840 | bytes 29360128 | tf_op jit(solution)/shard_map/pallas_call | solution.py:214
  824.5 2.8 convolution_convert_fusion.3
  827.3 9.3 slice_bitcast_fusion.5
  836.7 5.8 collective-permute-start.17
  842.5 27.6 %collective-permute-start.16 = (bf16[2,512,1024]{2,1,0:T(8,128)(2,1)}, bf16[2,512,1024]{2,1,0:T(8,128)(2,1)S(1)}, u32[]{:S(2)}, u32[]{:S(2)}) collective-permute-start(bf16[2,512,1024]{2,1,0:T(8,128)(2,1)} %get-tuple-element.64), channel_id=1, source_target_pairs={{0,2},{1,3},{2,4},{3,5},{4,6},{5,7},{6,8},{7,9},{8,10},{9,11},{10,... | collective-permute-start | bytes 6291464 | tf_op jit(solution)/shard_map/ppermute | solution.py:22
  870.1 22.2 %collective-permute-start.15 = (bf16[2,512,1024]{2,1,0:T(8,128)(2,1)}, bf16[2,512,1024]{2,1,0:T(8,128)(2,1)S(1)}, u32[]{:S(2)}, u32[]{:S(2)}) collective-permute-start(bf16[2,512,1024]{2,1,0:T(8,128)(2,1)} %get-tuple-element.65), channel_id=1, source_target_pairs={{0,1},{1,2},{2,3},{3,4},{4,5},{5,6},{6,7},{7,8},{8,9},{9,10},{10,1... | collective-permute-start | bytes 6291464 | tf_op jit(solution)/shard_map/ppermute | solution.py:22
  896.2 31.3 %collective-permute-done.16 = bf16[2,512,1024]{2,1,0:T(8,128)(2,1)S(1)} collective-permute-done((bf16[2,512,1024]{2,1,0:T(8,128)(2,1)}, bf16[2,512,1024]{2,1,0:T(8,128)(2,1)S(1)}, u32[]{:S(2)}, u32[]{:S(2)}) %collective-permute-start.16) | collective-permute-done | bytes 2097184 | tf_op jit(solution)/shard_map/ppermute | solution.py:22
  927.6 75.9 %collective-permute-done.15 = bf16[2,512,1024]{2,1,0:T(8,128)(2,1)S(1)} collective-permute-done((bf16[2,512,1024]{2,1,0:T(8,128)(2,1)}, bf16[2,512,1024]{2,1,0:T(8,128)(2,1)S(1)}, u32[]{:S(2)}, u32[]{:S(2)}) %collective-permute-start.15) | collective-permute-done | bytes 2097184 | tf_op jit(solution)/shard_map/ppermute | solution.py:22
  1003.5 37.7 %collective-permute-done.13 = bf16[2,512,1024]{2,1,0:T(8,128)(2,1)S(1)} collective-permute-done((bf16[2,512,1024]{2,1,0:T(8,128)(2,1)}, bf16[2,512,1024]{2,1,0:T(8,128)(2,1)S(1)}, u32[]{:S(2)}, u32[]{:S(2)}) %collective-permute-start.13) | collective-permute-done | bytes 2097184 | tf_op jit(solution)/shard_map/ppermute | solution.py:22
  1041.2 99.3 %collective-permute-done.12 = bf16[2,512,1024]{2,1,0:T(8,128)(2,1)S(1)} collective-permute-done((bf16[2,512,1024]{2,1,0:T(8,128)(2,1)}, bf16[2,512,1024]{2,1,0:T(8,128)(2,1)S(1)}, u32[]{:S(2)}, u32[]{:S(2)}) %collective-permute-start.12) | collective-permute-done | bytes 2097184 | tf_op jit(solution)/shard_map/ppermute | solution.py:22
  1140.4 5.1 fusion.9
  1145.5 2.0 copy-done.6
  1148.9 4.5 convolution_convert_fusion.2
  1155.8 3.3 convert_reduce_fusion
  1159.4 1.8 slice_reduce_fusion
  1161.2 4.6 fusion.10
  1165.8 4.8 fusion.26
  1170.7 47.3 %reduce-scatter.10.cloned.1.call-done = bf16[128,1024]{1,0:T(8,128)(2,1)} async-done(((bf16[1024,1024]{1,0:T(8,128)(2,1)}), bf16[128,1024]{1,0:T(8,128)(2,1)}) %reduce-scatter.10.cloned.1.call-update) | async-done | bytes 262160 | tf_op jit(solution)/shard_map/reduce_scatter | solution.py:264
  1218.0 90.7 %reduce-scatter.8.cloned.1.call-done = bf16[128,2048]{1,0:T(8,128)(2,1)} async-done(((bf16[1024,2048]{1,0:T(8,128)(2,1)}), bf16[128,2048]{1,0:T(8,128)(2,1)}) %reduce-scatter.8.cloned.1.call-update) | async-done | bytes 524304 | tf_op jit(solution)/shard_map/reduce_scatter | solution.py:264
  1308.7 152.9 %reduce-scatter.12.cloned.1.call-done = bf16[128,4096]{1,0:T(8,128)(2,1)} async-done(((bf16[1024,4096]{1,0:T(8,128)(2,1)}), bf16[128,4096]{1,0:T(8,128)(2,1)}) %reduce-scatter.12.cloned.1.call-update) | async-done | bytes 1048592 | tf_op jit(solution)/shard_map/reduce_scatter | solution.py:264
  1461.6 151.7 %reduce-scatter.14.cloned.1.call-done = bf16[512,1024]{1,0:T(8,128)(2,1)} async-done(((bf16[4096,1024]{1,0:T(8,128)(2,1)}), bf16[512,1024]{1,0:T(8,128)(2,1)}) %reduce-scatter.14.cloned.1.call-update) | async-done | bytes 1048592 | tf_op jit(solution)/shard_map/reduce_scatter | solution.py:264
  1613.4 35.6 %all-reduce = f32[8,1792]{1,0:T(8,128)S(1)} all-reduce(f32[8,1792]{1,0:T(8,128)S(1)} %constant_dynamic-update-slice_fusion.1), channel_id=3, replica_groups=mesh['rep'=4,'fsdp'=8] {'fsdp'}, use_global_device_ids=true, to_apply=%region_22.23.clone | all-reduce | flops 14336 | bytes 114688
  1649.7 5.8 psum.42
  1656.6 4.5 fusion.25
  1661.1 23.2 %all-reduce.4.cloned.1.call-done = (bf16[128,2048]{1,0:T(8,128)(2,1)}, bf16[128,1024]{1,0:T(8,128)(2,1)}, bf16[128,1024]{1,0:T(8,128)(2,1)}, bf16[128,4096]{1,0:T(8,128)(2,1)}, bf16[512,1024]{1,0:T(8,128)(2,1)}) async-done(((bf16[128,2048]{1,0:T(8,128)(2,1)}, bf16[128,1024]{1,0:T(8,128)(2,1)}, bf16[128,1024]{1,0:T(8,128)(2,1)}, bf16[128,4096]{1,0:T(8,128)(2,1)}, bf16[512,1024]{1,0:T(8,128)(2,1)}), ...) | async-done | bytes 3145744 | tf_op jit(solution)/shard_map/psum | solution.py:265
  1684.3 1.9 convert_element_type.160
  1686.2 2.8 convert_element_type.161
  1689.0 1.6 convert_element_type.162
  (185 shorter events, 31.5 us)
Async XLA Ops:
  7.2 3.0 copy-start.22
  7.2 3.2 copy-start.23
  7.2 3.4 copy-start.24
  7.2 3.6 copy-start.25
  7.2 3.9 copy-start.26
  7.2 4.1 copy-start.27
  7.3 4.3 copy-start.28
  7.3 4.5 copy-start.29
  7.3 4.7 copy-start.30
  7.3 4.9 copy-start.31
  7.3 5.1 copy-start.21
  7.3 38.1 %copy-start.3 = (bf16[512,1024]{1,0:T(8,128)(2,1)S(1)}, bf16[512,1024]{1,0:T(8,128)(2,1)}, u32[]{:S(2)}) copy-start(bf16[512,1024]{1,0:T(8,128)(2,1)} %param.18) | copy-start | bytes 3145732
  7.3 105.2 %all-gather.7.cloned.1.call-start = ((), (), s32[]{:S(2)}) async-start(), calls=%async_computation.5 | async-start | bytes 7077888 | tf_op jit(solution)/shard_map/all_gather | solution.py:260
  8.0 570.0 %all-gather.9.cloned.1.call-start = ((), (), s32[]{:S(2)}) async-start(), calls=%async_computation.6 | async-start | bytes 2359296 | tf_op jit(solution)/shard_map/all_gather | solution.py:260
  8.8 576.2 %all-gather.11.cloned.1.call-start = ((), (), s32[]{:S(2)}) async-start(), calls=%async_computation.7 | async-start | bytes 9437184 | tf_op jit(solution)/shard_map/all_gather | solution.py:260
  9.5 709.6 %all-gather.13.cloned.1.call-start = ((), (), s32[]{:S(2)}) async-start(), calls=%async_computation.8 | async-start | bytes 9437184 | tf_op jit(solution)/shard_map/all_gather | solution.py:260
  10.1 1160.5 %reduce-scatter.6.cloned.1.call-start = ((), (), s32[]{:S(2)}) async-start(), calls=%async_computation.9 | async-start | bytes 2359296 | tf_op jit(solution)/shard_map/reduce_scatter | solution.py:264
  118.6 4.8 copy-start.20
  120.1 209.7 %collective-permute-start.6 = (bf16[2,512,1024]{2,1,0:T(8,128)(2,1)}, bf16[2,512,1024]{2,1,0:T(8,128)(2,1)}, u32[]{:S(2)}, u32[]{:S(2)}) collective-permute-start(bf16[2,512,1024]{2,1,0:T(8,128)(2,1)} %pad_maximum_fusion), channel_id=1, source_target_pairs={{0,3},{1,4},{2,5},{3,6},{4,7},{5,8},{6,9},{7,10},{8,11},{9,12},{10... | collective-permute-start | bytes 6291464 | tf_op jit(solution)/shard_map/ppermute | solution.py:22
  123.4 51.6 %collective-permute-start = (s32[512]{0:T(512)S(1)}, s32[512]{0:T(512)S(1)}, u32[]{:S(2)}, u32[]{:S(2)}) collective-permute-start(s32[512]{0:T(512)S(1)} %subtract_select_fusion), channel_id=1, source_target_pairs={{0,3},{1,4},{2,5},{3,6},{4,7},{5,8},{6,9},{7,10},{8,11},{9,12},{10... | collective-permute-start | bytes 6152 | tf_op jit(solution)/shard_map/ppermute | solution.py:22
  126.8 53.0 %collective-permute-start.1 = (s32[512]{0:T(512)S(1)}, s32[512]{0:T(512)S(1)}, u32[]{:S(2)}, u32[]{:S(2)}) collective-permute-start(s32[512]{0:T(512)S(1)} %subtract_select_fusion), channel_id=1, source_target_pairs={{0,2},{1,3},{2,4},{3,5},{4,6},{5,7},{6,8},{7,9},{8,10},{9,11},{10,... | collective-permute-start | bytes 6152 | tf_op jit(solution)/shard_map/ppermute | solution.py:22
  129.2 52.0 %collective-permute-start.2 = (s32[512]{0:T(512)S(1)}, s32[512]{0:T(512)S(1)}, u32[]{:S(2)}, u32[]{:S(2)}) collective-permute-start(s32[512]{0:T(512)S(1)} %subtract_select_fusion), channel_id=1, source_target_pairs={{0,1},{1,2},{2,3},{3,4},{4,5},{5,6},{6,7},{7,8},{8,9},{9,10},{10,1... | collective-permute-start | bytes 6152 | tf_op jit(solution)/shard_map/ppermute | solution.py:22
  132.5 50.0 %collective-permute-start.3 = (s32[512]{0:T(512)S(1)}, s32[512]{0:T(512)S(1)}, u32[]{:S(2)}, u32[]{:S(2)}) collective-permute-start(s32[512]{0:T(512)S(1)} %subtract_select_fusion), channel_id=1, source_target_pairs={{1,0},{2,1},{3,2},{4,3},{5,4},{6,5},{7,6},{8,7},{9,8},{10,9},{11,1... | collective-permute-start | bytes 6152 | tf_op jit(solution)/shard_map/ppermute | solution.py:22
  175.0 160.9 %collective-permute-start.7 = (bf16[2,512,1024]{2,1,0:T(8,128)(2,1)}, bf16[2,512,1024]{2,1,0:T(8,128)(2,1)}, u32[]{:S(2)}, u32[]{:S(2)}) collective-permute-start(bf16[2,512,1024]{2,1,0:T(8,128)(2,1)} %pad_maximum_fusion), channel_id=1, source_target_pairs={{0,2},{1,3},{2,4},{3,5},{4,6},{5,7},{6,8},{7,9},{8,10},{9,11},{10,... | collective-permute-start | bytes 6291464 | tf_op jit(solution)/shard_map/ppermute | solution.py:22
  179.9 67.9 %collective-permute-start.4 = (s32[512]{0:T(512)S(1)}, s32[512]{0:T(512)S(1)}, u32[]{:S(2)}, u32[]{:S(2)}) collective-permute-start(s32[512]{0:T(512)S(1)} %subtract_select_fusion), channel_id=1, source_target_pairs={{2,0},{3,1},{4,2},{5,3},{6,4},{7,5},{8,6},{9,7},{10,8},{11,9},{12,... | collective-permute-start | bytes 6152 | tf_op jit(solution)/shard_map/ppermute | solution.py:22
  181.2 143.8 %collective-permute-start.5 = (s32[512]{0:T(512)S(1)}, s32[512]{0:T(512)S(1)}, u32[]{:S(2)}, u32[]{:S(2)}) collective-permute-start(s32[512]{0:T(512)S(1)} %subtract_select_fusion), channel_id=1, source_target_pairs={{3,0},{4,1},{5,2},{6,3},{7,4},{8,5},{9,6},{10,7},{11,8},{12,9},{13... | collective-permute-start | bytes 6152 | tf_op jit(solution)/shard_map/ppermute | solution.py:22
  182.5 155.2 %collective-permute-start.8 = (bf16[2,512,1024]{2,1,0:T(8,128)(2,1)}, bf16[2,512,1024]{2,1,0:T(8,128)(2,1)}, u32[]{:S(2)}, u32[]{:S(2)}) collective-permute-start(bf16[2,512,1024]{2,1,0:T(8,128)(2,1)} %pad_maximum_fusion), channel_id=1, source_target_pairs={{0,1},{1,2},{2,3},{3,4},{4,5},{5,6},{6,7},{7,8},{8,9},{9,10},{10,1... | collective-permute-start | bytes 6291464 | tf_op jit(solution)/shard_map/ppermute | solution.py:22
  325.1 128.1 %collective-permute-start.9 = (bf16[2,512,1024]{2,1,0:T(8,128)(2,1)}, bf16[2,512,1024]{2,1,0:T(8,128)(2,1)}, u32[]{:S(2)}, u32[]{:S(2)}) collective-permute-start(bf16[2,512,1024]{2,1,0:T(8,128)(2,1)} %pad_maximum_fusion), channel_id=1, source_target_pairs={{1,0},{2,1},{3,2},{4,3},{5,4},{6,5},{7,6},{8,7},{9,8},{10,9},{11,1... | collective-permute-start | bytes 6291464 | tf_op jit(solution)/shard_map/ppermute | solution.py:22
  327.7 199.6 %collective-permute-start.10 = (bf16[2,512,1024]{2,1,0:T(8,128)(2,1)}, bf16[2,512,1024]{2,1,0:T(8,128)(2,1)}, u32[]{:S(2)}, u32[]{:S(2)}) collective-permute-start(bf16[2,512,1024]{2,1,0:T(8,128)(2,1)} %pad_maximum_fusion), channel_id=1, source_target_pairs={{2,0},{3,1},{4,2},{5,3},{6,4},{7,5},{8,6},{9,7},{10,8},{11,9},{12,... | collective-permute-start | bytes 6291464 | tf_op jit(solution)/shard_map/ppermute | solution.py:22
  329.7 212.3 %copy-start.1 = (s32[3584,1]{1,0:T(8,128)}, s32[3584,1]{1,0:T(8,128)S(1)}, u32[]{:S(2)}) copy-start(s32[3584,1]{1,0:T(8,128)S(1)} %broadcast_in_dim.45.ck_ref) | copy-start | bytes 43012
  329.7 206.9 %collective-permute-start.11 = (bf16[2,512,1024]{2,1,0:T(8,128)(2,1)}, bf16[2,512,1024]{2,1,0:T(8,128)(2,1)S(1)}, u32[]{:S(2)}, u32[]{:S(2)}) collective-permute-start(bf16[2,512,1024]{2,1,0:T(8,128)(2,1)} %pad_maximum_fusion), channel_id=1, source_target_pairs={{3,0},{4,1},{5,2},{6,3},{7,4},{8,5},{9,6},{10,7},{11,8},{12,9},{13... | collective-permute-start | bytes 6291464 | tf_op jit(solution)/shard_map/ppermute | solution.py:22
  337.7 1.9 copy-start.11
  536.8 5.2 copy-start.18
  578.1 182.9 %copy-start = (f32[512,1024]{1,0:T(8,128)}, f32[512,1024]{1,0:T(8,128)S(1)}, u32[]{:S(2)}) copy-start(f32[512,1024]{1,0:T(8,128)S(1)} %get-tuple-element.28.o_ref) | copy-start | bytes 6291460
  583.3 1.3 copy-start.7
  585.0 14.1 copy-start.32
  597.1 2.0 copy-start.35
  719.1 11.7 copy-start.8
  728.7 2.1 copy-start.10
  738.0 10.4 copy-start.9
  738.0 10.4 copy-start.12
  738.0 10.4 copy-start.33
  738.1 10.4 copy-start.36
  761.0 1.0 copy-start.14
  764.6 3.3 copy-start.2
  767.9 56.6 %copy-start.4 = (bf16[512,1024]{1,0:T(8,128)(2,1)S(1)}, bf16[512,1024]{1,0:T(8,128)(2,1)}, u32[]{:S(2)}) copy-start(bf16[512,1024]{1,0:T(8,128)(2,1)} %param.18) | copy-start | bytes 3145732
  827.3 390.7 %reduce-scatter.10.cloned.1.call-start = ((), (), s32[]{:S(2)}) async-start(), calls=%async_computation.11 | async-start | bytes 2359296 | tf_op jit(solution)/shard_map/reduce_scatter | solution.py:264
  836.7 58.3 %collective-permute-start.17 = (bf16[2,512,1024]{2,1,0:T(8,128)(2,1)}, bf16[2,512,1024]{2,1,0:T(8,128)(2,1)S(1)}, u32[]{:S(2)}, u32[]{:S(2)}) collective-permute-start(bf16[2,512,1024]{2,1,0:T(8,128)(2,1)} %get-tuple-element.63), channel_id=1, source_target_pairs={{0,3},{1,4},{2,5},{3,6},{4,7},{5,8},{6,9},{7,10},{8,11},{9,12},{10... | collective-permute-start | bytes 6291464 | tf_op jit(solution)/shard_map/ppermute | solution.py:22
  842.5 466.2 %reduce-scatter.8.cloned.1.call-start = ((), (), s32[]{:S(2)}) async-start(), calls=%async_computation.10 | async-start | bytes 4718592 | tf_op jit(solution)/shard_map/reduce_scatter | solution.py:264
  842.5 85.1 %collective-permute-start.16 = (bf16[2,512,1024]{2,1,0:T(8,128)(2,1)}, bf16[2,512,1024]{2,1,0:T(8,128)(2,1)S(1)}, u32[]{:S(2)}, u32[]{:S(2)}) collective-permute-start(bf16[2,512,1024]{2,1,0:T(8,128)(2,1)} %get-tuple-element.64), channel_id=1, source_target_pairs={{0,2},{1,3},{2,4},{3,5},{4,6},{5,7},{6,8},{7,9},{8,10},{9,11},{10,... | collective-permute-start | bytes 6291464 | tf_op jit(solution)/shard_map/ppermute | solution.py:22
  870.1 133.4 %collective-permute-start.15 = (bf16[2,512,1024]{2,1,0:T(8,128)(2,1)}, bf16[2,512,1024]{2,1,0:T(8,128)(2,1)S(1)}, u32[]{:S(2)}, u32[]{:S(2)}) collective-permute-start(bf16[2,512,1024]{2,1,0:T(8,128)(2,1)} %get-tuple-element.65), channel_id=1, source_target_pairs={{0,1},{1,2},{2,3},{3,4},{4,5},{5,6},{6,7},{7,8},{8,9},{9,10},{10,1... | collective-permute-start | bytes 6291464 | tf_op jit(solution)/shard_map/ppermute | solution.py:22
  892.3 111.2 %collective-permute-start.14 = (bf16[2,512,1024]{2,1,0:T(8,128)(2,1)}, bf16[2,512,1024]{2,1,0:T(8,128)(2,1)S(1)}, u32[]{:S(2)}, u32[]{:S(2)}) collective-permute-start(bf16[2,512,1024]{2,1,0:T(8,128)(2,1)} %get-tuple-element.66), channel_id=1, source_target_pairs={{1,0},{2,1},{3,2},{4,3},{5,4},{6,5},{7,6},{8,7},{9,8},{10,9},{11,1... | collective-permute-start | bytes 6291464 | tf_op jit(solution)/shard_map/ppermute | solution.py:22
  893.6 147.5 %collective-permute-start.13 = (bf16[2,512,1024]{2,1,0:T(8,128)(2,1)}, bf16[2,512,1024]{2,1,0:T(8,128)(2,1)S(1)}, u32[]{:S(2)}, u32[]{:S(2)}) collective-permute-start(bf16[2,512,1024]{2,1,0:T(8,128)(2,1)} %get-tuple-element.67), channel_id=1, source_target_pairs={{2,0},{3,1},{4,2},{5,3},{6,4},{7,5},{8,6},{9,7},{10,8},{11,9},{12,... | collective-permute-start | bytes 6291464 | tf_op jit(solution)/shard_map/ppermute | solution.py:22
  894.9 245.5 %collective-permute-start.12 = (bf16[2,512,1024]{2,1,0:T(8,128)(2,1)}, bf16[2,512,1024]{2,1,0:T(8,128)(2,1)S(1)}, u32[]{:S(2)}, u32[]{:S(2)}) collective-permute-start(bf16[2,512,1024]{2,1,0:T(8,128)(2,1)} %get-tuple-element.62), channel_id=1, source_target_pairs={{3,0},{4,1},{5,2},{6,3},{7,4},{8,5},{9,6},{10,7},{11,8},{12,9},{13... | collective-permute-start | bytes 6291464 | tf_op jit(solution)/shard_map/ppermute | solution.py:22
  1145.5 2.1 copy-start.6
  1147.6 1.3 copy-start.5
  1153.4 308.2 %reduce-scatter.12.cloned.1.call-start = ((), (), s32[]{:S(2)}) async-start(), calls=%async_computation.12 | async-start | bytes 9437184 | tf_op jit(solution)/shard_map/reduce_scatter | solution.py:264
  1154.2 1.1 copy-start.34
  1154.2 459.1 %reduce-scatter.14.cloned.1.call-start = ((), (), s32[]{:S(2)}) async-start(), calls=%async_computation.13 | async-start | bytes 9437184 | tf_op jit(solution)/shard_map/reduce_scatter | solution.py:264
  1154.9 529.4 %all-reduce.4.cloned.1.call-start = ((), (), s32[]{:S(2)}) async-start(), calls=%async_computation.14 | async-start | bytes 6291456 | tf_op jit(solution)/shard_map/psum | solution.py:265
  1159.2 2.0 copy-start.16
  1684.3 4.6 copy-start.13
  1689.0 1.6 copy-start.17
  1689.0 1.6 copy-start.19
  (1 other events, 1.0 us)
Sparse Core Ops, SparseCore 0:
  10.3 102.1 all-gather.6
  114.6 97.2 all-gather.8
  214.1 275.1 all-gather.10
  491.3 227.8 all-gather.12
  827.4 314.6 reduce-scatter.5
  1145.5 72.4 reduce-scatter.9
  1221.6 87.0 reduce-scatter.7
  1312.8 148.7 reduce-scatter.11
  1465.3 148.0 reduce-scatter.13
  1616.1 68.1 all-reduce.3

commit v2 on v1

--- a/solution.py
+++ b/solution.py
@@ -71,13 +71,14 @@
 
 
 def attend_kernel(limits, q_ref, kv_ref, cq_ref, ck_ref, o_ref, lse_ref):
-    rows = q_ref.shape[0]
+    rows = q_ref.shape[1]
     step = K_TILE_FWD
+    query_block = pl.program_id(0)
     per_block = rows // step
     for tile in range(rows // Q_TILE):
         here = pl.ds(tile * Q_TILE, Q_TILE)
-        q_pair = two_heads(q_ref[here, :])
-        codes = twice(cq_ref[:, here])
+        q_pair = two_heads(q_ref[0, here, :])
+        codes = twice(cq_ref[0, :, here])
 
         def body(index, carry):
             peak, total, acc = carry
@@ -107,28 +108,34 @@
             jnp.zeros((1, 2 * Q_TILE), jnp.float32),
             jnp.zeros((HD, 2 * Q_TILE), jnp.float32),
         )
-        first = limits[2 * tile] // (step // K_TILE_BWD)
-        last = (limits[2 * tile + 1] + step // K_TILE_BWD - 1) // (step // K_TILE_BWD)
+        entry = 2 * (query_block * (rows // Q_TILE) + tile)
+        first = limits[entry] // (step // K_TILE_BWD)
+        last = (limits[entry + 1] + step // K_TILE_BWD - 1) // (step // K_TILE_BWD)
         peak, total, acc = lax.fori_loop(first, last, body, start)
         acc = acc / total
-        o_ref[here, :] = jnp.concatenate([acc[:, :Q_TILE], acc[:, Q_TILE:]], axis=0).T
+        o_ref[0, here, :] = jnp.concatenate([acc[:, :Q_TILE], acc[:, Q_TILE:]], axis=0).T
         lse_ref[0, :, pl.ds(tile * 2 * Q_TILE, 2 * Q_TILE)] = peak + jnp.log(total) * LOG2E
 
 
 def attend_back_kernel(
     limits, q_ref, kv_ref, go_ref, o_ref, lse_ref, cq_ref, ck_ref, dq_ref, dkv_ref, acc_ref
 ):
-    rows = q_ref.shape[0]
+    rows = q_ref.shape[1]
     step = K_TILE_BWD
+    query_block = pl.program_id(0)
     per_block = rows // step
     score_scale = HD ** (-0.5)
-    acc_ref[...] = jnp.zeros_like(acc_ref)
+
+    @pl.when(query_block == 0)
+    def _():
+        acc_ref[...] = jnp.zeros_like(acc_ref)
+
     for tile in range(rows // Q_TILE):
         here = pl.ds(tile * Q_TILE, Q_TILE)
-        q_pair = two_heads(q_ref[here, :])
-        go = go_ref[here, :]
+        q_pair = two_heads(q_ref[0, here, :])
+        go = go_ref[0, here, :]
         go_pair = two_heads(go)
-        inner = (go.astype(jnp.float32) * o_ref[here, :]).T
+        inner = (go.astype(jnp.float32) * o_ref[0, here, :]).T
         inner = jnp.concatenate(
             [
                 jnp.sum(inner[:HD, :], axis=0, keepdims=True),
@@ -137,7 +144,7 @@
             axis=1,
         )
         lse = lse_ref[0, :, pl.ds(tile * 2 * Q_TILE, 2 * Q_TILE)]
-        codes = twice(cq_ref[:, here])
+        codes = twice(cq_ref[0, :, here])
 
         def body(index, dq):
             block = index // per_block
@@ -161,108 +168,158 @@
             )
             return dq + part
 
+        entry = 2 * (query_block * (rows // Q_TILE) + tile)
         dq = lax.fori_loop(
-            limits[2 * tile],
-            limits[2 * tile + 1],
+            limits[entry],
+            limits[entry + 1],
             body,
             jnp.zeros((2 * HD, Q_TILE), jnp.float32),
         )
-        dq_ref[here, :] = (dq * score_scale).T.astype(jnp.bfloat16)
-    dkv_ref[:, 0, :, :] = (acc_ref[:, 0, :, :] * score_scale).astype(jnp.bfloat16)
-    dkv_ref[:, 1, :, :] = acc_ref[:, 1, :, :].astype(jnp.bfloat16)
+        dq_ref[0, here, :] = (dq * score_scale).T.astype(jnp.bfloat16)
+
+    @pl.when(query_block == pl.num_programs(0) - 1)
+    def _():
+        dkv_ref[:, 0, :, :] = (acc_ref[:, 0, :, :] * score_scale).astype(jnp.bfloat16)
+        dkv_ref[:, 1, :, :] = acc_ref[:, 1, :, :].astype(jnp.bfloat16)
 
 
 def attend(limits, queries, near, own_codes, near_codes):
-    rows, width = queries.shape
-    blocks = near.shape[0]
-    pairs = width // (2 * HD)
-    lanes = 2 * HD
-    column = pl.BlockSpec((rows, lanes), lambda p, lim: (0, p))
+    blocks, rows, lanes = queries.shape
+    column = pl.BlockSpec((1, rows, lanes), lambda b, lim: (b, 0, 0))
     return pl.pallas_call(
         attend_kernel,
         grid_spec=pltpu.PrefetchScalarGridSpec(
             num_scalar_prefetch=1,
-            grid=(pairs,),
+            grid=(blocks,),
             in_specs=[
                 column,
-                pl.BlockSpec((blocks, 2, rows, lanes), lambda p, lim: (0, 0, 0, p)),
-                pl.BlockSpec((1, rows), lambda p, lim: (0, 0)),
-                pl.BlockSpec((blocks * rows, 1), lambda p, lim: (0, 0)),
+                pl.BlockSpec(near.shape, lambda b, lim: (0, 0, 0, 0)),
+                pl.BlockSpec((1, 1, rows), lambda b, lim: (b, 0, 0)),
+                pl.BlockSpec((near_codes.shape[0], 1), lambda b, lim: (0, 0)),
             ],
-            out_specs=[column, pl.BlockSpec((1, 1, 2 * rows), lambda p, lim: (p, 0, 0))],
+            out_specs=[column, pl.BlockSpec((1, 1, 2 * rows), lambda b, lim: (b, 0, 0))],
         ),
         out_shape=[
-            jax.ShapeDtypeStruct((rows, width), jnp.float32),
-            jax.ShapeDtypeStruct((pairs, 1, 2 * rows), jnp.float32),
+            jax.ShapeDtypeStruct((blocks, rows, lanes), jnp.float32),
+            jax.ShapeDtypeStruct((blocks, 1, 2 * rows), jnp.float32),
         ],
-        compiler_params=pltpu.CompilerParams(vmem_limit_bytes=48 * 2**20),
+        compiler_params=pltpu.CompilerParams(vmem_limit_bytes=50 * 2**20),
         cost_estimate=pl.CostEstimate(
-            flops=16 * rows * rows * blocks * width // 2,
-            bytes_accessed=2 * blocks * 2 * rows * width,
+            flops=64 * rows * rows * blocks * 4 * lanes,
+            bytes_accessed=16 * blocks * rows * lanes,
             transcendentals=0,
         ),
-    )(limits, queries, near, own_codes[None, :], near_codes[:, None])
+    )(limits, queries, near, own_codes[:, None, :], near_codes[:, None])
 
 
 def attend_back(limits, queries, near, g_out, out, lse, own_codes, near_codes):
-    rows, width = queries.shape
-    blocks = near.shape[0]
-    pairs = width // (2 * HD)
-    lanes = 2 * HD
-    column = pl.BlockSpec((rows, lanes), lambda p, lim: (0, p))
-    window = pl.BlockSpec((blocks, 2, rows, lanes), lambda p, lim: (0, 0, 0, p))
+    blocks, rows, lanes = queries.shape
+    column = pl.BlockSpec((1, rows, lanes), lambda b, lim: (b, 0, 0))
+    window = pl.BlockSpec(near.shape, lambda b, lim: (0, 0, 0, 0))
     return pl.pallas_call(
         attend_back_kernel,
         grid_spec=pltpu.PrefetchScalarGridSpec(
             num_scalar_prefetch=1,
-            grid=(pairs,),
+            grid=(blocks,),
             in_specs=[
                 column,
                 window,
                 column,
                 column,
-                pl.BlockSpec((1, 1, 2 * rows), lambda p, lim: (p, 0, 0)),
-                pl.BlockSpec((1, rows), lambda p, lim: (0, 0)),
-                pl.BlockSpec((blocks * rows, 1), lambda p, lim: (0, 0)),
+                pl.BlockSpec((1, 1, 2 * rows), lambda b, lim: (b, 0, 0)),
+                pl.BlockSpec((1, 1, rows), lambda b, lim: (b, 0, 0)),
+                pl.BlockSpec((near_codes.shape[0], 1), lambda b, lim: (0, 0)),
             ],
             out_specs=[column, window],
-            scratch_shapes=[pltpu.VMEM((blocks, 2, rows, lanes), jnp.float32)],
+            scratch_shapes=[pltpu.VMEM(near.shape, jnp.float32)],
         ),
         out_shape=[
-            jax.ShapeDtypeStruct((rows, width), jnp.bfloat16),
-            jax.ShapeDtypeStruct((blocks, 2, rows, width), jnp.bfloat16),
+            jax.ShapeDtypeStruct((blocks, rows, lanes), jnp.bfloat16),
+            jax.ShapeDtypeStruct(near.shape, jnp.bfloat16),
         ],
-        compiler_params=pltpu.CompilerParams(vmem_limit_bytes=48 * 2**20),
+        compiler_params=pltpu.CompilerParams(vmem_limit_bytes=50 * 2**20),
         cost_estimate=pl.CostEstimate(
-            flops=40 * rows * rows * blocks * width // 2,
-            bytes_accessed=4 * blocks * 2 * rows * width,
+            flops=128 * rows * rows * blocks * 4 * lanes,
+            bytes_accessed=32 * blocks * rows * lanes,
             transcendentals=0,
         ),
-    )(limits, queries, near, g_out, out, lse, own_codes[None, :], near_codes[:, None])
+    )(limits, queries, near, g_out, out, lse, own_codes[:, None, :], near_codes[:, None])
 
 
 def tile_limits(own_codes, near_codes):
-    same = own_codes[:, None] == near_codes[None, :]
-    queries = own_codes.shape[0] // Q_TILE
-    count = near_codes.shape[0] // K_TILE_BWD
-    touched = jnp.any(same.reshape(queries, Q_TILE, count, K_TILE_BWD), axis=(1, 3))
-    number = jnp.arange(count, dtype=jnp.int32)[None, :]
-    first = jnp.min(jnp.where(touched, number, count), axis=1)
-    last = jnp.max(jnp.where(touched, number + 1, 0), axis=1)
-    return jnp.stack([first, last], axis=1).reshape(-1)
-
-
-def side_offsets():
-    return [offset for offset in range(-REACH, REACH + 1) if offset != 0]
+    blocks, rows = own_codes.shape
+    window = (2 * REACH + 1) * rows
+    seen = jnp.stack([near_codes[b * rows : b * rows + window] for b in range(blocks)])
+    same = own_codes[:, :, None] == seen[:, None, :]
+    tiles, count = rows // Q_TILE, window // K_TILE_BWD
+    touched = jnp.any(same.reshape(blocks, tiles, Q_TILE, count, K_TILE_BWD), axis=(2, 4))
+    number = jnp.arange(count, dtype=jnp.int32)[None, None, :]
+    first = jnp.min(jnp.where(touched, number, count), axis=2)
+    last = jnp.max(jnp.where(touched, number + 1, 0), axis=2)
+    shift = (jnp.arange(blocks, dtype=jnp.int32) * (rows // K_TILE_BWD))[:, None]
+    return jnp.stack([first + shift, last + shift], axis=2).reshape(-1)
+
+
+def regrouped(pieces, size):
+    count = lax.axis_size("fsdp")
+    groups = None
+    if count != size:
+        groups = [list(range(at, at + size)) for at in range(0, count, size)]
+    return lax.all_to_all(pieces, "fsdp", 0, 0, axis_index_groups=groups)
+
+
+def with_partner(value):
+    count = lax.axis_size("rep")
+    return lax.ppermute(value, "rep", [(at, at + 1 - 2 * (at % 2)) for at in range(count)])
+
+
+def is_second():
+    return lax.rem(lax.axis_index("rep"), 2) == 1
+
+
+def halves(matrix):
+    middle = matrix.shape[1] // 2
+    left, right = matrix[:, :middle], matrix[:, middle:]
+    second = is_second()
+    return jnp.where(second, right, left), jnp.where(second, left, right)
+
+
+def joined(mine, other):
+    second = is_second()
+    return jnp.concatenate(
+        [jnp.where(second, other, mine), jnp.where(second, mine, other)], axis=1
+    )
 
 
 def gathered_rows(weight):
-    return lax.all_gather(weight, "fsdp", axis=0, tiled=True)
-
-
-def reduced_rows(grad):
-    part = lax.psum_scatter(grad.astype(jnp.bfloat16), "fsdp", scatter_dimension=0, tiled=True)
-    return lax.psum(part, "rep").astype(jnp.float32)
+    mine, _ = halves(weight)
+    whole = lax.all_gather(mine, "fsdp", axis=0, tiled=True)
+    return joined(whole, with_partner(whole))
+
+
+def reduced_half(grad):
+    mine, other = halves(grad)
+    total = (as_float(mine) + as_float(with_partner(other))).astype(jnp.bfloat16)
+    return lax.psum_scatter(total, "fsdp", scatter_dimension=0, tiled=True)
+
+
+def finished(parts):
+    count = lax.axis_size("rep")
+    groups = [list(range(core, count, 2)) for core in range(2)]
+    flat = jnp.concatenate([part.reshape(-1, 128) for part in parts], axis=0)
+    mine = lax.psum(flat, "rep", axis_index_groups=groups)
+    other = with_partner(mine)
+    results = []
+    at = 0
+    for part in parts:
+        size = part.size // 128
+        results.append(
+            joined(mine[at : at + size].reshape(part.shape), other[at : at + size].reshape(part.shape)).astype(
+                jnp.float32
+            )
+        )
+        at += size
+    return results
 
 
 def local(
@@ -287,17 +344,12 @@
 ):
     both = ("rep", "fsdp")
     fsdp = lax.axis_size("fsdp")
-    model_width = tokens.shape[1]
-    tok_rows = tokens.shape[0]
-    offsets = side_offsets()
+    tok_rows, model_width = tokens.shape
+    lanes = 2 * HD
+    group = model_width // lanes
 
     place = lax.axis_index(both) * tok_rows + lax.iota(jnp.int32, tok_rows)
-    own_codes = jnp.where(segment >= 0, segment + 1, -1 - place)
-    side_codes = {offset: passed_along(own_codes, both, -offset) for offset in offsets}
-    side_codes[0] = own_codes
-    near_codes = jnp.concatenate([side_codes[o] for o in range(-REACH, REACH + 1)])
-    limits = tile_limits(own_codes, near_codes)
-
+    codes = as_float(jnp.where(segment >= 0, segment + 1, -1 - place))
     vectors = (
         attn_norm_gain,
         attn_norm_bias,
@@ -311,7 +363,8 @@
         mlp_scale,
         hidden_bias,
     )
-    packed_vectors = as_float(lax.all_gather(jnp.concatenate(vectors), "fsdp", axis=0))
+    to_gather = jnp.concatenate([as_float(vector) for vector in vectors] + [codes])
+    packed_vectors = lax.all_gather(to_gather, "fsdp", axis=0)
     whole = []
     at = 0
     for vector in vectors:
@@ -331,6 +384,16 @@
         scale_two,
         bias_hidden,
     ) = whole
+    first_of_group = lax.axis_index("fsdp") // group * group
+    own_codes = lax.dynamic_slice_in_dim(packed_vectors[:, at:], first_of_group, group, 0)
+    near_codes = jnp.concatenate(
+        [
+            passed_along(own_codes[group - REACH :], both, group),
+            own_codes,
+            passed_along(own_codes[:REACH], both, -group),
+        ]
+    ).reshape(-1)
+    limits = tile_limits(own_codes, near_codes)
     w_qkv = gathered_rows(qkv_weight)
     w_proj = gathered_rows(proj_weight)
     w_hidden = gathered_rows(hidden_weight)
@@ -339,17 +402,21 @@
     inputs = as_float(tokens)
     normed_one, inverse_one = layer_norm_parts(inputs)
     first_in = (normed_one * gain_one + shift_one).astype(jnp.bfloat16)
-    kv_plain = plain_dot(first_in, w_qkv[:, model_width:])
-    packed = jnp.stack(
-        [kv_plain[:, :model_width], kv_plain[:, model_width:] + bias_value]
-    ).astype(jnp.bfloat16)
-    sides = {offset: passed_along(packed, both, -offset) for offset in offsets}
-    sides[0] = packed
-    queries = (plain_dot(first_in, w_qkv[:, :model_width]) + bias_query).astype(jnp.bfloat16)
-    near = jnp.stack([sides[o] for o in range(-REACH, REACH + 1)])
-
+    bias_row = jnp.concatenate([bias_query, jnp.zeros_like(bias_query), bias_value])
+    mixed = (plain_dot(first_in, w_qkv) + bias_row).astype(jnp.bfloat16)
+    mixed = mixed.reshape(tok_rows, 3, group, lanes).transpose(2, 1, 0, 3)
+    mixed = regrouped(mixed, group)
+    queries, packed = mixed[:, 0], mixed[:, 1:]
+    near = jnp.concatenate(
+        [
+            passed_along(packed[group - REACH :], both, group),
+            packed,
+            passed_along(packed[:REACH], both, -group),
+        ]
+    )
     attended_wide, lse = attend(limits, queries, near, own_codes, near_codes)
-    attended = attended_wide.astype(jnp.bfloat16)
+    attended = regrouped(attended_wide.astype(jnp.bfloat16), group)
+    attended = attended.transpose(1, 0, 2).reshape(tok_rows, model_width)
     branch_one = plain_dot(attended, w_proj) + bias_proj
     middle = inputs + scale_one * branch_one
     normed_two, inverse_two = layer_norm_parts(middle)
@@ -384,28 +451,31 @@
     g_attended, hidden_weight_grad, proj_weight_grad = lax.optimization_barrier(
         (g_attended, hidden_weight_grad, proj_weight_grad)
     )
-    output_weight_out = reduced_rows(output_weight_grad)
-    hidden_weight_out = reduced_rows(hidden_weight_grad)
-    proj_weight_out = reduced_rows(proj_weight_grad)
-
+    output_weight_part = reduced_half(output_weight_grad)
+    hidden_weight_part = reduced_half(hidden_weight_grad)
+    proj_weight_part = reduced_half(proj_weight_grad)
+
+    g_heads = regrouped(g_attended.reshape(tok_rows, group, lanes).transpose(1, 0, 2), group)
     g_query, g_near = attend_back(
-        limits, queries, near, g_attended, attended_wide, lse, own_codes, near_codes
-    )
-    arrived = [passed_along(g_near[offset + REACH], both, offset) for offset in offsets]
-    query_weight_grad = dot_first_t(first_in, g_query).astype(jnp.bfloat16)
-    query_bias_grad = column_sum(g_query)
-    g_first = dot_second_t(g_query, w_qkv[:, :model_width])
-    g_kv = as_float(g_near[REACH])
-    for piece in arrived:
-        g_kv = g_kv + as_float(piece)
-    value_bias_grad = jnp.sum(g_kv[1], axis=0)
-    g_keys, g_values = g_kv[0].astype(jnp.bfloat16), g_kv[1].astype(jnp.bfloat16)
-    g_kv_low = jnp.concatenate([g_keys, g_values], axis=1)
-    kv_weight_grad = dot_first_t(first_in, g_kv_low).astype(jnp.bfloat16)
-    g_first = g_first + dot_second_t(g_kv_low, w_qkv[:, model_width:])
-    qkv_weight_out = jnp.concatenate(
-        [reduced_rows(query_weight_grad), reduced_rows(kv_weight_grad)], axis=1
-    )
+        limits, queries, near, g_heads, attended_wide, lse, own_codes, near_codes
+    )
+    g_query, g_near, output_weight_part = lax.optimization_barrier(
+        (g_query, g_near, output_weight_part)
+    )
+    from_next = passed_along(g_near[group + REACH :], both, group)
+    from_last = passed_along(g_near[:REACH], both, -group)
+    g_own = as_float(g_near[REACH : group + REACH])
+    filler = jnp.zeros((group - REACH,) + g_own.shape[1:], jnp.float32)
+    g_own = g_own + jnp.concatenate([as_float(from_next), filler])
+    g_own = g_own + jnp.concatenate([filler, as_float(from_last)])
+    g_mixed = jnp.concatenate([g_query[:, None], g_own.astype(jnp.bfloat16)], axis=1)
+    g_mixed = regrouped(g_mixed, group).transpose(2, 1, 0, 3).reshape(tok_rows, 3 * model_width)
+    qkv_weight_grad = dot_first_t(first_in, g_mixed).astype(jnp.bfloat16)
+    qkv_weight_part = reduced_half(qkv_weight_grad)
+    mixed_sums = column_sum(g_mixed)
+    query_bias_grad = mixed_sums[:model_width]
+    value_bias_grad = mixed_sums[2 * model_width :]
+    g_first = dot_second_t(g_mixed, w_qkv)
     gain_one_grad = jnp.sum(g_first * normed_one, axis=0)
     shift_one_grad = jnp.sum(g_first, axis=0)
     input_grad = g_middle + layer_norm_back(g_first * gain_one, normed_one, inverse_one)
@@ -427,6 +497,9 @@
     small_sum = lax.psum(
         lax.psum_scatter(small_rows, "fsdp", scatter_dimension=0, tiled=True), "rep"
     ).reshape(-1)
+    qkv_weight_out, proj_weight_out, hidden_weight_out, output_weight_out = finished(
+        (qkv_weight_part, proj_weight_part, hidden_weight_part, output_weight_part)
+    )
     owned = []
     at = 0
     for vector in small:

time: 1710 us -> 1010 us (0.59)
  waiting for transfers between devices: 1200 us -> 520 us
  starting transfers between devices: 151 us -> 40.1 us
  other arithmetic: 29.7 us -> 97.1 us
  Pallas kernels: 92.6 us -> 111 us
    ppermute x18 -> x6, waiting for transfers between devices: 556 us -> 0.69 us  [passed_along(): lax.ppermute(value, axis, [(source, source + steps) for source in range(l...]
    reduce_scatter x5 -> x4, waiting for transfers between devices: 443 us -> 155 us  [reduced_half(): return lax.psum_scatter(total, 'fsdp', scatter_dimension=0, tiled=True)]
    all_to_all x0 -> x4, waiting for transfers between devices: none -> 196 us  [regrouped(): return lax.all_to_all(pieces, 'fsdp', 0, 0, axis_index_groups=groups)]
    ppermute x18 -> x6, starting transfers between devices: 150 us -> 13.9 us  [passed_along(): lax.ppermute(value, axis, [(source, source + steps) for source in range(l...]
    all_gather x4, waiting for transfers between devices: 179 us -> 121 us  [gathered_rows(): whole = lax.all_gather(mine, 'fsdp', axis=0, tiled=True)]
    select_n x1 -> x15, other arithmetic: 0.01 us -> 36.5 us  [the longest x7 21.2 us: joined(): jnp.where(second, other, mine)]
    convert_element_type x3 -> x10, other arithmetic: 6.2 us -> 28.3 us  [the longest x4 20.4 us: reduced_half(): (as_float(mine) + as_float(with_partner(other))).astype(jnp.bfloat16)]
    psum x1, waiting for transfers between devices: 23.2 us -> 41.2 us  [finished(): mine = lax.psum(flat, 'rep', axis_index_groups=groups)]
  transfers between devices with their start and end apart: 28 -> 28, of which waited for: 16 -> 12; matrix products, arithmetic and copies ran while one was open for 5% -> 16% of each run, Pallas kernels for 2% -> 11%
where the time goes in v2:
time: 1010 us; the launch traced here: 997 us
  waiting for transfers between devices  520 us (51%)
  Pallas kernels  111 us (11%)
  other arithmetic  97.1 us (10%)
  matrix products  87.8 us (9%)
  blocking collectives  75 us (7%)
  local copies, waits for them, and re-layouts  51.3 us (5%)
  starting transfers between devices  40.1 us (4%)
  between operations  15.1 us (1%)
    all_to_all x4, waiting for transfers between devices, regrouped(): return lax.all_to_all(pieces, 'fsdp', 0, 0, axis_index_groups=groups)  196 us
    reduce_scatter x4, waiting for transfers between devices, reduced_half(): return lax.psum_scatter(total, 'fsdp', scatter_dimension=0, tiled=True)  155 us
    all_gather x4, waiting for transfers between devices, gathered_rows(): whole = lax.all_gather(mine, 'fsdp', axis=0, tiled=True)  121 us
    pallas_call x1, Pallas kernels, attend_back(): pl.pallas_call(attend_back_kernel, grid_spec=pltpu.PrefetchScalarGridSpec...  63.1 us
    pallas_call x1, Pallas kernels, attend(): pl.pallas_call(attend_kernel, grid_spec=pltpu.PrefetchScalarGridSpec(num_...  47.8 us
    psum x1, waiting for transfers between devices, finished(): mine = lax.psum(flat, 'rep', axis_index_groups=groups)  41.2 us
    unnamed x1, blocking collectives  38.2 us
    dot_general x4, matrix products, dot_second_t(): lax.dot_general(first_op, second_op, (((1,), (1,)), ((), ())), preferred_...  34.1 us
  transfers between devices with their start and end apart: 28, of which 12 were waited for; matrix products, arithmetic and copies ran while one was open for 16% of the time, Pallas kernels for 11%

profile of v2, /device:TPU:0, one launch (start us, length us, event | category | flops | bytes accessed | tf_op | source)
XLA Modules:
  0.0 997.1 jit_solution(5661793809672893653)
XLA Ops:
  7.4 2.0 slice_select_fusion.2
  11.2 2.1 slice_select_fusion.1
  14.3 59.7 %all-gather.7.cloned.1.call-done = bf16[1024,1536]{1,0:T(8,128)(2,1)} async-done(((bf16[128,1536]{1,0:T(8,128)(2,1)}), bf16[1024,1536]{1,0:T(8,128)(2,1)}) %all-gather.7.cloned.1.call-update) | async-done | bytes 3145744 | tf_op jit(solution)/shard_map/all_gather | solution.py:296
  74.2 30.7 %all-gather.1 = f32[8,1,2304]{2,1,0:T(1,128)S(1)} all-gather(f32[1,1,2304]{2,1,0:T(1,128)S(1)} %reshape.315), channel_id=2, replica_groups=mesh['rep'=4,'fsdp'=8] {'fsdp'}, dimensions={0}, use_global_device_ids=true | all-gather | bytes 82944 | tf_op jit(solution)/shard_map/all_gather | solution.py:367
  106.2 2.3 broadcast_select_fusion.8
  111.2 5.4 add_convert_fusion.3
  116.6 3.2 copy.61
  119.8 2.8 copy.62
  122.6 3.7 all-to-all-start
  127.6 3.0 collective-permute-start
  132.9 13.3 %compare_reduce_fusion = pred[8,2,14]{2,1,0:T(4,128)(4,1)S(1)} fusion(f32[8,14,256]{2,1,0:T(8,128)S(1)} %constant_dynamic-update-slice_fusion.1, f32[8,2,256]{2,1,0:T(2,128)S(1)} %copy.57), kind=kLoop, calls=%fused_computation | loop fusion | flops 29359904 | bytes 131296 | tf_op jit(solution)/shard_map/reduce_or | solution.py:255
  146.7 95.7 %all-to-all-done = bf16[8,3,512,128]{3,2,1,0:T(8,128)(2,1)S(1)} async-done(((bf16[8,3,512,128]{3,2,1,0:T(8,128)(2,1)}), bf16[8,3,512,128]{3,2,1,0:T(8,128)(2,1)S(1)}, u32[]{:S(2)}, u32[]{:S(2)}) %all-to-all-start) | async-done | bytes 3145760 | tf_op jit(solution)/shard_map/all_to_all | solution.py:268
  245.0 3.9 collective-permute-start.3
  249.2 2.4 copy.73
  251.6 3.1 broadcast_select_fusion.11
  255.0 61.6 %all-gather.13.cloned.1.call-done = bf16[4096,512]{1,0:T(8,128)(2,1)} async-done(((bf16[512,512]{1,0:T(8,128)(2,1)}), bf16[4096,512]{1,0:T(8,128)(2,1)}) %all-gather.13.cloned.1.call-update) | async-done | bytes 4194320 | tf_op jit(solution)/shard_map/all_gather | solution.py:296
  318.5 3.1 pad_maximum_fusion.9.kv_ref
  321.5 47.8 %shard_map.305 = (f32[8,512,128]{2,1,0:T(8,128)S(1)}, f32[8,1,1024]{2,1,0:T(1,128)S(1)}) custom-call(s32[32]{0:T(128)S(1)} %reshape.294.limits, bf16[8,512,128]{2,1,0:T(8,128)(2,1)S(1)} %slice_bitcast_fusion.q_ref, bf16[14,2,512,128]{3,2,1,0:T(8,128)(2,1)} %pad_maximum_fusion.9.kv_ref, f32[8,1,512]{2,1,0:T(1,128)S(1)} %broadcast_in_dim.49.cq_ref, ...), custom_call_target="tpu_custom_call" | custom-call | flops 68719476736 | bytes 8388608 | tf_op jit(solution)/shard_map/pallas_call | solution.py:189
  370.6 4.7 all-to-all-start.1
  375.3 6.6 broadcast_select_fusion.5
  382.5 5.3 broadcast_select_fusion.2
  387.8 13.9 %all-to-all-done.1 = bf16[8,512,128]{2,1,0:T(8,128)(2,1)} async-done(((bf16[8,512,128]{2,1,0:T(8,128)(2,1)}), bf16[8,512,128]{2,1,0:T(8,128)(2,1)}, u32[]{:S(2)}, u32[]{:S(2)}) %all-to-all-start.1) | async-done | bytes 1048608 | tf_op jit(solution)/shard_map/all_to_all | solution.py:268
  401.7 2.3 copy.64
  404.0 3.2 fusion.42
  408.1 10.9 %fusion.4 = (bf16[512,4096]{1,0:T(8,128)(2,1)}, bf16[512,4096]{1,0:T(8,128)(2,1)}) fusion(f32[4096]{0:T(1024)S(1)} %bitcast.115, bf16[1024,2048]{1,0:T(8,128)(2,1)S(1)} %copy-done.12, bf16[1024,2048]{1,0:T(8,128)(2,1)S(1)} %copy-done.11, f32[512,1024]{1,0:T(8,128)S(1)} %get-tuple-element.62, f32[1024]{0:T(1024)S(1)} %get-tuple-element.90, ...), kind=kOutput, calls=%fused_computation.6 | convolution fusion | flops 4339531776 | bytes 18903040 | tf_op jit(solution)/shard_map/dot_general | solution.py:40
  419.0 7.2 convolution_convert_fusion.1
  426.2 11.5 %multiply_convert_fusion = bf16[512,4096]{1,0:T(8,128)(2,1)} fusion(bf16[512,4096]{1,0:T(8,128)(2,1)} %get-tuple-element.33, bf16[4096,512]{1,0:T(8,128)(2,1)} %get-tuple-element.66, bf16[4096,512]{1,0:T(8,128)(2,1)S(1)} %copy-done.10, bf16[512,1024]{1,0:T(8,128)(2,1)S(1)} %copy-done.33, f32[1024]{0:T(1024)S(1)} %get-tuple-element.88), kind=kOutput, calls=%fused_computation.12 | convolution fusion | flops 4319608832 | bytes 17829888 | tf_op jit(solution)/shard_map/dot_general | solution.py:50
  437.7 10.4 %multiply_reduce_fusion = (f32[1024]{0:T(1024)}, f32[512]{0:T(512)S(1)}, f32[512]{0:T(512)S(1)}, f32[1024]{0:T(1024)}, f32[512,1024]{1,0:T(8,128)}) fusion(f32[512,1024]{1,0:T(8,128)S(1)} %get-tuple-element.62, f32[512]{0:T(512)S(1)} %add_rsqrt_fusion, f32[512]{0:T(512)S(1)} %broadcast_multiply_fusion.4, f32[1024]{0:T(1024)S(1)} %get-tuple-element.91, ...), kind=kOutput, calls=%fused_computation.63 | convolution fusion | flops 4316460032 | bytes 16797696 | tf_op jit(solution)/shard_map/dot_general | solution.py:50
  448.1 2.3 broadcast_select_fusion
  451.5 11.1 %fusion.24 = (f32[1024]{0:T(1024)}, f32[1024]{0:T(1024)}, bf16[512,1024]{1,0:T(8,128)(2,1)}, f32[1024]{0:T(1024)}, f32[512,1024]{1,0:T(8,128)S(1)}) fusion(bf16[512,1024]{1,0:T(8,128)(2,1)S(1)} %copy-done.33, f32[1024]{0:T(1024)S(1)} %copy-done.30, f32[1024]{0:T(1024)S(1)} %get-tuple-element.88, f32[512,1024]{1,0:T(8,128)S(1)} %get-tuple-element.62, ...), kind=kOutput, calls=%fused_computation.59 | convolution fusion | flops 4323275776 | bytes 23105536 | tf_op jit(solution)/shard_map/dot_general | solution.py:40
  464.6 2.3 convolution_convert_fusion.4
  467.0 2.6 convolution_convert_fusion.3
  469.6 7.4 convolution_convert_fusion
  478.8 3.6 all-to-all-start.2
  482.8 5.1 broadcast_select_fusion.3
  488.0 6.9 add_convert_fusion.1
  494.8 22.0 %all-to-all-done.2.go_ref = bf16[8,512,128]{2,1,0:T(8,128)(2,1)S(1)} async-done(((bf16[8,512,128]{2,1,0:T(8,128)(2,1)}), bf16[8,512,128]{2,1,0:T(8,128)(2,1)S(1)}, u32[]{:S(2)}, u32[]{:S(2)}) %all-to-all-start.2) | async-done | bytes 1048608 | tf_op jit(solution)/shard_map/all_to_all | solution.py:268
  516.9 63.1 %shard_map.306 = (bf16[8,512,128]{2,1,0:T(8,128)(2,1)S(1)}, bf16[14,2,512,128]{3,2,1,0:T(8,128)(2,1)}) custom-call(s32[32]{0:T(128)S(1)} %reshape.294.limits, bf16[8,512,128]{2,1,0:T(8,128)(2,1)S(1)} %slice_bitcast_fusion.q_ref, bf16[14,2,512,128]{3,2,1,0:T(8,128)(2,1)} %pad_maximum_fusion.9.kv_ref, bf16[8,512,128]{2,1,0:T(8,128)(2,1)S(1)} %all-to-all-done.2.go_ref, ...), custom_call_target="tpu_custom_call" | custom-call | flops 137438953472 | bytes 16777216 | tf_op jit(solution)/shard_map/pallas_call | solution.py:219
  579.9 5.6 reduce-scatter.5.cloned.1.call-done
  588.5 3.1 collective-permute-start.9
  594.2 1.9 pad_maximum_fusion.10
  596.1 4.5 all-to-all-start.3
  600.7 3.2 add_convert_fusion.5
  604.0 7.5 add_convert_fusion
  611.5 64.9 %all-to-all-done.3 = bf16[8,3,512,128]{3,2,1,0:T(8,128)(2,1)S(1)} async-done(((bf16[8,3,512,128]{3,2,1,0:T(8,128)(2,1)}), bf16[8,3,512,128]{3,2,1,0:T(8,128)(2,1)S(1)}, u32[]{:S(2)}, u32[]{:S(2)}) %all-to-all-start.3) | async-done | bytes 3145760 | tf_op jit(solution)/shard_map/all_to_all | solution.py:268
  676.4 2.8 copy.68
  679.3 6.0 convolution_convert_fusion.2
  685.6 5.2 collective-permute-start.11
  690.8 5.3 collective-permute-done.11
  696.1 2.9 add_convert_fusion.2
  700.2 3.2 convert_reduce_fusion
  703.4 1.6 reshape.311
  705.1 2.1 reshape.313
  707.2 84.4 %reduce-scatter.11.cloned.1.call-done = bf16[128,2048]{1,0:T(8,128)(2,1)} async-done(((bf16[1024,2048]{1,0:T(8,128)(2,1)}), bf16[128,2048]{1,0:T(8,128)(2,1)}) %reduce-scatter.11.cloned.1.call-update) | async-done | bytes 524304 | tf_op jit(solution)/shard_map/reduce_scatter | solution.py:303
  791.6 2.1 reshape.312
  793.7 9.8 fusion.21
  805.1 64.7 %reduce-scatter.7.cloned.1.call-done = bf16[128,1536]{1,0:T(8,128)(2,1)} async-done(((bf16[1024,1536]{1,0:T(8,128)(2,1)}), bf16[128,1536]{1,0:T(8,128)(2,1)}) %reduce-scatter.7.cloned.1.call-update) | async-done | bytes 393232 | tf_op jit(solution)/shard_map/reduce_scatter | solution.py:303
  871.3 2.5 pad_maximum_fusion.12
  883.4 41.2 %all-reduce.5.cloned.1.call-done = bf16[6144,128]{1,0:T(8,128)(2,1)} async-done(((bf16[6144,128]{1,0:T(8,128)(2,1)}), bf16[6144,128]{1,0:T(8,128)(2,1)}) %all-reduce.5.cloned.1.call-update) | async-done | bytes 1572880 | tf_op jit(solution)/shard_map/psum | solution.py:310
  926.5 38.2 %all-reduce.2 = f32[8,1792]{1,0:T(8,128)S(1)} all-reduce(f32[8,1792]{1,0:T(8,128)} %constant_dynamic-update-slice_fusion.9), channel_id=4, replica_groups=mesh['rep'=4,'fsdp'=8] {'fsdp'}, use_global_device_ids=true, to_apply=%region_22.23.clone | all-reduce | flops 14336 | bytes 114688
  965.3 6.1 psum.14
  973.9 3.6 fusion.20
  981.4 1.7 broadcast_select_fusion.13
  985.5 1.7 maximum_convert_fusion.3
  (244 shorter events, 58.1 us)
Async XLA Ops:
  7.2 6.1 copy-start.20
  7.2 66.8 %all-gather.7.cloned.1.call-start = ((), (), s32[]{:S(2)}) async-start(), calls=%async_computation.8 | async-start | bytes 3538944 | tf_op jit(solution)/shard_map/all_gather | solution.py:296
  7.3 7.0 copy-start.34
  7.3 7.0 copy-start.35
  7.3 7.0 copy-start.36
  7.3 66.7 %copy-start.37 = (bf16[128]{0:T(256)(128)(2,1)S(1)}, bf16[128]{0:T(256)(128)(2,1)}, u32[]{:S(2)}) copy-start(bf16[128]{0:T(256)(128)(2,1)} %param.25) | copy-start | bytes 772
  7.3 66.7 %copy-start.38 = (bf16[128]{0:T(256)(128)(2,1)S(1)}, bf16[128]{0:T(256)(128)(2,1)}, u32[]{:S(2)}) copy-start(bf16[128]{0:T(256)(128)(2,1)} %param.27) | copy-start | bytes 772
  7.3 66.7 %copy-start.39 = (bf16[128]{0:T(256)(128)(2,1)S(1)}, bf16[128]{0:T(256)(128)(2,1)}, u32[]{:S(2)}) copy-start(bf16[128]{0:T(256)(128)(2,1)} %param.28) | copy-start | bytes 772
  7.3 66.7 %copy-start.40 = (bf16[128]{0:T(256)(128)(2,1)S(1)}, bf16[128]{0:T(256)(128)(2,1)}, u32[]{:S(2)}) copy-start(bf16[128]{0:T(256)(128)(2,1)} %param.29) | copy-start | bytes 772
  7.3 66.7 %copy-start.41 = (bf16[128]{0:T(256)(128)(2,1)S(1)}, bf16[128]{0:T(256)(128)(2,1)}, u32[]{:S(2)}) copy-start(bf16[128]{0:T(256)(128)(2,1)} %param.30) | copy-start | bytes 772
  7.3 66.8 %copy-start.42 = (bf16[128]{0:T(256)(128)(2,1)S(1)}, bf16[128]{0:T(256)(128)(2,1)}, u32[]{:S(2)}) copy-start(bf16[128]{0:T(256)(128)(2,1)} %param.34) | copy-start | bytes 772
  7.3 66.8 %copy-start.43 = (bf16[128]{0:T(256)(128)(2,1)S(1)}, bf16[128]{0:T(256)(128)(2,1)}, u32[]{:S(2)}) copy-start(bf16[128]{0:T(256)(128)(2,1)} %param.35) | copy-start | bytes 772
  7.4 66.8 %copy-start.32 = (bf16[512]{0:T(512)(128)(2,1)S(1)}, bf16[512]{0:T(512)(128)(2,1)}, u32[]{:S(2)}) copy-start(bf16[512]{0:T(512)(128)(2,1)} %param.32) | copy-start | bytes 3076
  7.4 66.8 %copy-start.31 = (s32[512]{0:T(512)S(1)}, s32[512]{0:T(512)}, u32[]{:S(2)}) copy-start(s32[512]{0:T(512)} %param.19) | copy-start | bytes 6148
  7.4 98.2 %copy-start.3 = (bf16[512,1024]{1,0:T(8,128)(2,1)S(1)}, bf16[512,1024]{1,0:T(8,128)(2,1)}, u32[]{:S(2)}) copy-start(bf16[512,1024]{1,0:T(8,128)(2,1)} %param.18) | copy-start | bytes 3145732
  9.4 122.3 %all-gather.9.cloned.1.call-start = ((), (), s32[]{:S(2)}) async-start(), calls=%async_computation.9 | async-start | bytes 1179648 | tf_op jit(solution)/shard_map/all_gather | solution.py:296
  11.1 243.6 %all-gather.11.cloned.1.call-start = ((), (), s32[]{:S(2)}) async-start(), calls=%async_computation.10 | async-start | bytes 4718592 | tf_op jit(solution)/shard_map/all_gather | solution.py:296
  13.3 303.3 %all-gather.13.cloned.1.call-start = ((), (), s32[]{:S(2)}) async-start(), calls=%async_computation.11 | async-start | bytes 4718592 | tf_op jit(solution)/shard_map/all_gather | solution.py:296
  74.0 32.2 %collective-permute-start.2 = (bf16[1024,1536]{1,0:T(8,128)(2,1)}, bf16[1024,1536]{1,0:T(8,128)(2,1)S(1)}, u32[]{:S(2)}, u32[]{:S(2)}) collective-permute-start(bf16[1024,1536]{1,0:T(8,128)(2,1)} %all-gather.7.cloned.1.call-done), channel_id=1, source_target_pairs={{0,8},{8,0},{16,24},{24,16},{1,9},{9,1},{17,25},{25,17},{2,10},{10... | collective-permute-start | bytes 9437192 | tf_op jit(solution)/shard_map/ppermute | solution.py:273
  105.5 3.0 copy-start.24
  105.5 3.0 copy-start.28
  122.6 119.7 %all-to-all-start = ((bf16[8,3,512,128]{3,2,1,0:T(8,128)(2,1)}), bf16[8,3,512,128]{3,2,1,0:T(8,128)(2,1)S(1)}, u32[]{:S(2)}, u32[]{:S(2)}) async-start(bf16[8,3,512,128]{3,2,1,0:T(8,128)(2,1)} %bitcast.100), calls=%async_computation | async-start | bytes 6291456 | tf_op jit(solution)/shard_map/all_to_all | solution.py:268
  126.3 4.5 collective-permute-start.1
  127.6 3.8 collective-permute-start
  131.7 119.9 %collective-permute-start.5 = (bf16[1024,512]{1,0:T(8,128)(2,1)}, bf16[1024,512]{1,0:T(8,128)(2,1)}, u32[]{:S(2)}, u32[]{:S(2)}) collective-permute-start(bf16[1024,512]{1,0:T(8,128)(2,1)} %all-gather.9.cloned.1.call-done), channel_id=1, source_target_pairs={{0,8},{8,0},{16,24},{24,16},{1,9},{9,1},{17,25},{25,17},{2,10},{10... | collective-permute-start | bytes 3145736 | tf_op jit(solution)/shard_map/ppermute | solution.py:273
  242.3 74.2 %copy-start.2 = (bf16[8,3,512,128]{3,2,1,0:T(8,128)(2,1)}, bf16[8,3,512,128]{3,2,1,0:T(8,128)(2,1)S(1)}, u32[]{:S(2)}) copy-start(bf16[8,3,512,128]{3,2,1,0:T(8,128)(2,1)S(1)} %all-to-all-done) | copy-start | bytes 9437188
  243.7 74.3 %collective-permute-start.4 = (bf16[3,2,512,128]{3,2,1,0:T(8,128)(2,1)}, bf16[3,2,512,128]{3,2,1,0:T(8,128)(2,1)}, u32[]{:S(2)}, u32[]{:S(2)}) collective-permute-start(bf16[3,2,512,128]{3,2,1,0:T(8,128)(2,1)} %get-tuple-element.82), channel_id=1, source_target_pairs={{8,0},{9,1},{10,2},{11,3},{12,4},{13,5},{14,6},{15,7},{16,8},{17,9... | collective-permute-start | bytes 2359304 | tf_op jit(solution)/shard_map/ppermute | solution.py:22
  245.0 73.1 %collective-permute-start.3 = (bf16[3,2,512,128]{3,2,1,0:T(8,128)(2,1)}, bf16[3,2,512,128]{3,2,1,0:T(8,128)(2,1)}, u32[]{:S(2)}, u32[]{:S(2)}) collective-permute-start(bf16[3,2,512,128]{3,2,1,0:T(8,128)(2,1)} %get-tuple-element.81), channel_id=1, source_target_pairs={{0,8},{1,9},{2,10},{3,11},{4,12},{5,13},{6,14},{7,15},{8,16},{9,17... | collective-permute-start | bytes 2359304 | tf_op jit(solution)/shard_map/ppermute | solution.py:22
  254.7 120.6 %collective-permute-start.6 = (bf16[1024,2048]{1,0:T(8,128)(2,1)}, bf16[1024,2048]{1,0:T(8,128)(2,1)}, u32[]{:S(2)}, u32[]{:S(2)}) collective-permute-start(bf16[1024,2048]{1,0:T(8,128)(2,1)} %all-gather.11.cloned.1.call-done), channel_id=1, source_target_pairs={{0,8},{8,0},{16,24},{24,16},{1,9},{9,1},{17,25},{25,17},{2,10},{10... | collective-permute-start | bytes 12582920 | tf_op jit(solution)/shard_map/ppermute | solution.py:273
  316.6 65.4 %collective-permute-start.7 = (bf16[4096,512]{1,0:T(8,128)(2,1)}, bf16[4096,512]{1,0:T(8,128)(2,1)}, u32[]{:S(2)}, u32[]{:S(2)}) collective-permute-start(bf16[4096,512]{1,0:T(8,128)(2,1)} %all-gather.13.cloned.1.call-done), channel_id=1, source_target_pairs={{0,8},{8,0},{16,24},{24,16},{1,9},{9,1},{17,25},{25,17},{2,10},{10... | collective-permute-start | bytes 12582920 | tf_op jit(solution)/shard_map/ppermute | solution.py:273
  369.3 12.6 %copy-start = (f32[8,512,128]{2,1,0:T(8,128)}, f32[8,512,128]{2,1,0:T(8,128)S(1)}, u32[]{:S(2)}) copy-start(f32[8,512,128]{2,1,0:T(8,128)S(1)} %get-tuple-element.31.o_ref) | copy-start | bytes 6291460
  370.6 31.1 %all-to-all-start.1 = ((bf16[8,512,128]{2,1,0:T(8,128)(2,1)}), bf16[8,512,128]{2,1,0:T(8,128)(2,1)}, u32[]{:S(2)}, u32[]{:S(2)}) async-start(bf16[8,512,128]{2,1,0:T(8,128)(2,1)} %convert_element_type.174), calls=%async_computation.1 | async-start | bytes 2097152 | tf_op jit(solution)/shard_map/all_to_all | solution.py:268
  375.3 7.2 copy-start.9
  382.5 21.5 %copy-start.4 = (bf16[512,1024]{1,0:T(8,128)(2,1)S(1)}, bf16[512,1024]{1,0:T(8,128)(2,1)}, u32[]{:S(2)}) copy-start(bf16[512,1024]{1,0:T(8,128)(2,1)} %param.18) | copy-start | bytes 3145732
  382.5 21.5 %copy-start.13 = (bf16[1024,512]{1,0:T(8,128)(2,1)S(1)}, bf16[1024,512]{1,0:T(8,128)(2,1)}, u32[]{:S(2)}) copy-start(bf16[1024,512]{1,0:T(8,128)(2,1)} %get-tuple-element.86) | copy-start | bytes 3145732
  404.0 3.5 copy-start.11
  404.0 4.1 copy-start.12
  408.1 10.9 %copy-start.33 = (bf16[512,1024]{1,0:T(8,128)(2,1)S(1)}, bf16[512,1024]{1,0:T(8,128)(2,1)}, u32[]{:S(2)}) copy-start(bf16[512,1024]{1,0:T(8,128)(2,1)} %param.20) | copy-start | bytes 3145732
  419.0 7.2 copy-start.10
  426.2 21.9 %copy-start.1 = (bf16[4096,1024]{1,0:T(8,128)(2,1)}, bf16[4096,1024]{1,0:T(8,128)(2,1)S(1)}, u32[]{:S(2)}) copy-start(bf16[4096,1024]{1,0:T(8,128)(2,1)S(1)} %convolution_convert_fusion.1) | copy-start | bytes 25165828
  448.1 3.4 copy-start.30
  450.4 37.5 %collective-permute-start.8 = (bf16[4096,512]{1,0:T(8,128)(2,1)}, bf16[4096,512]{1,0:T(8,128)(2,1)}, u32[]{:S(2)}, u32[]{:S(2)}) collective-permute-start(bf16[4096,512]{1,0:T(8,128)(2,1)} %broadcast_select_fusion), channel_id=1, source_target_pairs={{0,8},{8,0},{16,24},{24,16},{1,9},{9,1},{17,25},{25,17},{2,10},{10... | collective-permute-start | bytes 12582920 | tf_op jit(solution)/shard_map/ppermute | solution.py:273
  462.6 4.3 copy-start.7
  469.6 7.4 copy-start.21
  478.8 38.1 %all-to-all-start.2 = ((bf16[8,512,128]{2,1,0:T(8,128)(2,1)}), bf16[8,512,128]{2,1,0:T(8,128)(2,1)S(1)}, u32[]{:S(2)}, u32[]{:S(2)}) async-start(bf16[8,512,128]{2,1,0:T(8,128)(2,1)} %bitcast.19), calls=%async_computation.2 | async-start | bytes 2097152 | tf_op jit(solution)/shard_map/all_to_all | solution.py:268
  482.4 103.2 %reduce-scatter.5.cloned.1.call-start = ((), (), s32[]{:S(2)}) async-start(), calls=%async_computation.12 | async-start | bytes 4718592 | tf_op jit(solution)/shard_map/reduce_scatter | solution.py:303
  487.9 116.1 %collective-permute-start.13 = (bf16[1024,2048]{1,0:T(8,128)(2,1)}, bf16[1024,2048]{1,0:T(8,128)(2,1)}, u32[]{:S(2)}, u32[]{:S(2)}) collective-permute-start(bf16[1024,2048]{1,0:T(8,128)(2,1)} %broadcast_select_fusion.3), channel_id=1, source_target_pairs={{0,8},{8,0},{16,24},{24,16},{1,9},{9,1},{17,25},{25,17},{2,10},{10... | collective-permute-start | bytes 12582920 | tf_op jit(solution)/shard_map/ppermute | solution.py:273
  579.9 11.7 %copy-start.6 = (bf16[1024,1024]{1,0:T(8,128)(2,1)S(1)}, bf16[1024,1024]{1,0:T(8,128)(2,1)}, u32[]{:S(2)}) copy-start(bf16[1024,1024]{1,0:T(8,128)(2,1)} %convolution_convert_fusion.3) | copy-start | bytes 6291460
  585.6 8.2 copy-start.17
  587.2 6.5 collective-permute-start.10
  588.5 5.2 collective-permute-start.9
  592.7 8.0 collective-permute-start.12
  596.1 80.3 %all-to-all-start.3 = ((bf16[8,3,512,128]{3,2,1,0:T(8,128)(2,1)}), bf16[8,3,512,128]{3,2,1,0:T(8,128)(2,1)S(1)}, u32[]{:S(2)}, u32[]{:S(2)}) async-start(bf16[8,3,512,128]{3,2,1,0:T(8,128)(2,1)} %pad_maximum_fusion.10), calls=%async_computation.4 | async-start | bytes 6291456 | tf_op jit(solution)/shard_map/all_to_all | solution.py:268
  600.6 102.8 %reduce-scatter.9.cloned.1.call-start = ((), (), s32[]{:S(2)}) async-start(), calls=%async_computation.14 | async-start | bytes 1179648 | tf_op jit(solution)/shard_map/reduce_scatter | solution.py:303
  604.0 187.6 %reduce-scatter.11.cloned.1.call-start = ((), (), s32[]{:S(2)}) async-start(), calls=%async_computation.15 | async-start | bytes 4718592 | tf_op jit(solution)/shard_map/reduce_scatter | solution.py:303
  611.5 258.4 %reduce-scatter.7.cloned.1.call-start = ((), (), s32[]{:S(2)}) async-start(), calls=%async_computation.13 | async-start | bytes 3538944 | tf_op jit(solution)/shard_map/reduce_scatter | solution.py:303
  676.4 2.8 copy-start.25
  676.4 2.8 copy-start.27
  676.4 2.8 copy-start.29
  685.6 10.5 %collective-permute-start.11 = (bf16[1024,1536]{1,0:T(8,128)(2,1)S(1)}, bf16[1024,1536]{1,0:T(8,128)(2,1)S(1)}, u32[]{:S(2)}, u32[]{:S(2)}) collective-permute-start(bf16[1024,1536]{1,0:T(8,128)(2,1)S(1)} %broadcast_select_fusion.6), channel_id=1, source_target_pairs={{0,8},{8,0},{16,24},{24,16},{1,9},{9,1},{17,25},{25,17},{2,10},{10... | collective-permute-start | bytes 9437192 | tf_op jit(solution)/shard_map/ppermute | solution.py:273
  699.0 225.6 %all-reduce.5.cloned.1.call-start = ((), (), s32[]{:S(2)}) async-start(), calls=%async_computation.16 | async-start | bytes 3145728 | tf_op jit(solution)/shard_map/psum | solution.py:310
  805.1 168.7 %copy-start.5 = (bf16[512,1024]{1,0:T(8,128)(2,1)S(1)}, bf16[512,1024]{1,0:T(8,128)(2,1)}, u32[]{:S(2)}) copy-start(bf16[512,1024]{1,0:T(8,128)(2,1)} %param.18) | copy-start | bytes 3145732
  805.1 168.7 %copy-start.8 = (f32[512,1024]{1,0:T(8,128)S(1)}, f32[512,1024]{1,0:T(8,128)}, u32[]{:S(2)}) copy-start(f32[512,1024]{1,0:T(8,128)} %copy-done.7) | copy-start | bytes 6291460
  924.6 52.9 %collective-permute-start.14 = (bf16[6144,128]{1,0:T(8,128)(2,1)}, bf16[6144,128]{1,0:T(8,128)(2,1)}, u32[]{:S(2)}, u32[]{:S(2)}) collective-permute-start(bf16[6144,128]{1,0:T(8,128)(2,1)} %all-reduce.5.cloned.1.call-done), channel_id=1, source_target_pairs={{0,8},{8,0},{16,24},{24,16},{1,9},{9,1},{17,25},{25,17},{2,10},{10... | collective-permute-start | bytes 4718600 | tf_op jit(solution)/shard_map/ppermute | solution.py:273
  (10 other events, 21.8 us)
Sparse Core Ops, SparseCore 0:
  10.8 63.1 all-gather.6
  76.7 38.9 all-gather.8
  118.4 122.3 all-gather.10
  243.4 73.1 all-gather.12
  495.0 90.5 reduce-scatter.4
  605.5 95.4 reduce-scatter.8
  704.6 86.9 reduce-scatter.10
  795.6 74.2 reduce-scatter.6
  873.9 50.6 all-reduce.4
